TPU v7x, 256 devices: a whole 4x4x8 slice. The times are simulated.
256 devices in a mesh: row: 32 (over y, x, core), col: 8 (over z).
Axes of the slice: x: 4, y: 4, z: 8, core: 2. Of those that a mesh axis runs over, the one named last changes fastest.
Arguments:
- tokens: bfloat16 [1024, 8192], P(None, 'row'), may hold values from -6 to 6
- gate_weight: bfloat16 [8192, 14336], P('row', 'col'), may hold values from -0.0625 to 0.0625
- up_weight: bfloat16 [8192, 14336], P('row', 'col'), may hold values from -0.0625 to 0.0625
- down_weight: bfloat16 [14336, 8192], P('col', 'row'), may hold values from -0.046875 to 0.046875
- cotangent: bfloat16 [1024, 8192], P(None, 'row'), may hold values from -6 to 6
Outputs:
- output: bfloat16 [1024, 8192], P(None, 'row')
- tokens_grad: bfloat16 [1024, 8192], P(None, 'row')
- gate_grad: bfloat16 [8192, 14336], P('row', 'col')
- up_grad: bfloat16 [8192, 14336], P('row', 'col')
- down_grad: bfloat16 [14336, 8192], P('col', 'row')
All inputs are finite; a program needn't handle non-finite values.
Results may differ from a plain program's by a relative error of at most 0.035.
Values may be sent and summed in bfloat16 or wider, within the bound.
A program may use at most 64 MiB of HBM per device.

v0:
```python
import jax
import jax.numpy as jnp
from jax import lax
from jax.sharding import PartitionSpec as P


def times_transposed(left, right):
    return lax.dot_general(
        left, right, (((1,), (1,)), ((), ())), preferred_element_type=jnp.float32
    )


def transposed_times(left, right):
    return lax.dot_general(
        left, right, (((0,), (0,)), ((), ())), preferred_element_type=jnp.float32
    )


def pre_grads(hidden_grad, gate, up):
    gate_f = gate.astype(jnp.float32)
    up_f = up.astype(jnp.float32)
    sig = jax.nn.sigmoid(gate_f)
    gate_pre = (hidden_grad * up_f * sig * (1.0 + gate_f * (1.0 - sig))).astype(jnp.bfloat16)
    up_pre = (hidden_grad * gate_f * sig).astype(jnp.bfloat16)
    return (gate_pre, up_pre)


def activate(gate, up):
    gate_f = gate.astype(jnp.float32)
    return (gate_f * jax.nn.sigmoid(gate_f) * up.astype(jnp.float32)).astype(jnp.bfloat16)


def per_device(tokens, gate_weight, up_weight, down_weight, cotangent):
    hidden_cols = gate_weight.shape[1]
    block = tokens
    summed = lax.psum_scatter(
        jnp.concatenate(
            [
                jnp.dot(block, gate_weight, preferred_element_type=jnp.float32),
                jnp.dot(block, up_weight, preferred_element_type=jnp.float32),
            ],
            axis=1,
        ).astype(jnp.bfloat16),
        "row",
        scatter_dimension=0,
        tiled=True,
    ).astype(jnp.float32)
    gate = summed[:, :hidden_cols].astype(jnp.bfloat16)
    up = summed[:, hidden_cols:].astype(jnp.bfloat16)
    hidden_all = lax.all_gather(activate(gate, up), "row", axis=0, tiled=True)
    block = cotangent
    hidden_grad = lax.psum_scatter(
        times_transposed(block, down_weight).astype(jnp.bfloat16),
        "row",
        scatter_dimension=0,
        tiled=True,
    ).astype(jnp.float32)
    hidden_grad = hidden_grad.astype(jnp.bfloat16).astype(jnp.float32)
    gate_pre, up_pre = pre_grads(hidden_grad, gate, up)
    gate_pre_all, up_pre_all = (
        lax.all_gather(gate_pre, "row", axis=0, tiled=True),
        lax.all_gather(up_pre, "row", axis=0, tiled=True),
    )
    output_part = jnp.dot(hidden_all, down_weight, preferred_element_type=jnp.float32)
    output = lax.psum(output_part.astype(jnp.bfloat16), "col")
    down_grad = transposed_times(hidden_all, cotangent).astype(jnp.bfloat16)
    gate_grad = transposed_times(tokens, gate_pre_all).astype(jnp.bfloat16)
    up_grad = transposed_times(tokens, up_pre_all).astype(jnp.bfloat16)
    input_part = times_transposed(gate_pre_all, gate_weight) + times_transposed(
        up_pre_all, up_weight
    )
    tokens_grad = lax.psum(input_part.astype(jnp.bfloat16), "col")
    return (output, tokens_grad, gate_grad, up_grad, down_grad)


def solution(mesh):
    return jax.shard_map(
        per_device,
        mesh=mesh,
        in_specs=(
            P(None, "row"),
            P("row", "col"),
            P("row", "col"),
            P("col", "row"),
            P(None, "row"),
        ),
        out_specs=(
            P(None, "row"),
            P(None, "row"),
            P("row", "col"),
            P("row", "col"),
            P("col", "row"),
        ),
        check_vma=False,
    )
```

profile of v0, /device:TPU:1, one launch (start us, length us, event | category | flops | bytes accessed | tf_op | source)
XLA Modules:
  0.0 451.0 jit_solution(102983443683301761)
XLA Ops:
  7.2 1.1 copy-done
  8.4 4.1 convolution_convert_fusion
  12.5 1.0 copy-done.1
  13.5 2.4 convolution_convert_fusion.2
  15.9 3.0 convolution_convert_fusion.1
  18.9 5.5 %pad_maximum_fusion = bf16[1024,3584]{1,0:T(8,128)(2,1)} fusion(bf16[1024,1792]{1,0:T(8,128)(2,1)} %convolution_convert_fusion.1, bf16[1024,1792]{1,0:T(8,128)(2,1)S(1)} %convolution_convert_fusion.2), kind=kLoop, calls=%fused_computation | loop fusion | flops 14680064 | bytes 14680064 | tf_op jit(solution)/shard_map/concatenate | solution.py:37
  24.5 79.0 %reduce-scatter.5.cloned.1.call-done = bf16[32,1792]{1,0:T(8,128)(2,1)} async-done(((bf16[1024,1792]{1,0:T(8,128)(2,1)}), bf16[32,1792]{1,0:T(8,128)(2,1)}) %reduce-scatter.5.cloned.1.call-update) | async-done | bytes 114704 | tf_op jit(solution)/shard_map/reduce_scatter | solution.py:52
  103.5 100.0 %reduce-scatter.3.cloned.1.call-done = bf16[32,3584]{1,0:T(8,128)(2,1)} async-done(((bf16[1024,3584]{1,0:T(8,128)(2,1)}), bf16[32,3584]{1,0:T(8,128)(2,1)}) %reduce-scatter.3.cloned.1.call-update) | async-done | bytes 229392 | tf_op jit(solution)/shard_map/reduce_scatter | solution.py:36
  203.6 1.9 fusion.12
  206.1 0.5 all-gather.8.cloned.1.call-update
  206.7 52.2 %all-gather.4.cloned.1.call-done = bf16[1024,1792]{1,0:T(8,128)(2,1)} async-done(((bf16[32,1792]{1,0:T(8,128)(2,1)}), bf16[1024,1792]{1,0:T(8,128)(2,1)}) %all-gather.4.cloned.1.call-update) | async-done | bytes 3670032 | tf_op jit(solution)/shard_map/all_gather | solution.py:50
  258.8 3.9 convolution_convert_fusion.6
  262.8 49.1 %all-gather.6.cloned.1.call-done = bf16[1024,1792]{1,0:T(8,128)(2,1)} async-done(((bf16[32,1792]{1,0:T(8,128)(2,1)}), bf16[1024,1792]{1,0:T(8,128)(2,1)}) %all-gather.6.cloned.1.call-update) | async-done | bytes 3670032 | tf_op jit(solution)/shard_map/all_gather | solution.py:61
  311.9 4.2 fusion.13
  316.0 48.9 %all-gather.8.cloned.1.call-done = bf16[1024,1792]{1,0:T(8,128)(2,1)} async-done(((bf16[32,1792]{1,0:T(8,128)(2,1)}), bf16[1024,1792]{1,0:T(8,128)(2,1)}) %all-gather.8.cloned.1.call-update) | async-done | bytes 3670032 | tf_op jit(solution)/shard_map/all_gather | solution.py:62
  364.9 4.3 fusion.2
  369.2 3.2 fusion.1
  372.5 1.4 copy.11
  373.8 3.3 fusion
  377.1 1.4 copy.10
  378.5 4.2 convolution_convert_fusion.3
  382.7 57.7 %all-reduce.3.cloned.1.call-done = (bf16[1024,256]{1,0:T(8,128)(2,1)}, bf16[1024,256]{1,0:T(8,128)(2,1)}) async-done(((bf16[1024,256]{1,0:T(8,128)(2,1)}, bf16[1024,256]{1,0:T(8,128)(2,1)}), (bf16[1024,256]{1,0:T(8,128)(2,1)}, bf16[1024,256]{1,0:T(8,128)(2,1)})) %all-reduce.3.cloned.1.call-update) | async-done | bytes 1048592 | tf_op jit(solution)/shard_map/psum | solution.py:65
  440.4 1.9 copy.14
  442.3 1.9 copy.15
  (21 shorter events, 0.9 us)
Async XLA Ops:
  7.2 1.2 copy-start
  7.2 96.3 %reduce-scatter.5.cloned.1.call-start = ((), (), s32[]{:S(2)}) async-start(), calls=%async_computation.4 | async-start | bytes 3784704 | tf_op jit(solution)/shard_map/reduce_scatter | solution.py:52
  12.5 1.0 copy-start.1
  12.5 191.1 %reduce-scatter.3.cloned.1.call-start = ((), (), s32[]{:S(2)}) async-start(), calls=%async_computation.2 | async-start | bytes 7569408 | tf_op jit(solution)/shard_map/reduce_scatter | solution.py:36
  13.5 2.4 copy-start.4
  24.5 287.4 %copy-start.3 = (bf16[256,1792]{1,0:T(8,128)(2,1)S(1)}, bf16[256,1792]{1,0:T(8,128)(2,1)}, u32[]{:S(2)}) copy-start(bf16[256,1792]{1,0:T(8,128)(2,1)} %param.6) | copy-start | bytes 2752516
  24.5 234.3 %all-gather.4.cloned.1.call-start = ((), (), s32[]{:S(2)}) async-start(), calls=%async_computation.3 | async-start | bytes 3784704 | tf_op jit(solution)/shard_map/all_gather | solution.py:50
  205.4 106.4 %all-gather.6.cloned.1.call-start = ((), (), s32[]{:S(2)}) async-start(), calls=%async_computation.5 | async-start | bytes 3784704 | tf_op jit(solution)/shard_map/all_gather | solution.py:61
  206.0 158.9 %all-gather.8.cloned.1.call-start = ((), (), s32[]{:S(2)}) async-start(), calls=%async_computation.6 | async-start | bytes 3784704 | tf_op jit(solution)/shard_map/all_gather | solution.py:62
  206.6 233.8 %all-reduce.3.cloned.1.call-start = ((), (), s32[]{:S(2)}) async-start(), calls=%async_computation.7 | async-start | bytes 2097152 | tf_op jit(solution)/shard_map/psum | solution.py:65
  262.8 102.2 %copy-start.5 = (bf16[256,1792]{1,0:T(8,128)(2,1)S(1)}, bf16[256,1792]{1,0:T(8,128)(2,1)}, u32[]{:S(2)}) copy-start(bf16[256,1792]{1,0:T(8,128)(2,1)} %param.7) | copy-start | bytes 2752516
  373.8 4.6 %copy-start.2 = (bf16[1024,256]{1,0:T(8,128)(2,1)S(1)}, bf16[1024,256]{1,0:T(8,128)(2,1)}, u32[]{:S(2)}) copy-start(bf16[1024,256]{1,0:T(8,128)(2,1)} %param.9) | copy-start | bytes 1572868
Sparse Core Ops, SparseCore 0:
  12.6 90.8 reduce-scatter.4
  108.1 95.3 reduce-scatter.2
  206.7 52.0 all-gather.3
  261.8 50.0 all-gather.5
  314.9 50.0 all-gather.7
  369.4 71.0 all-reduce.2
where the time goes:
time: 455 us; the launch traced here: 451 us
  waiting for transfers between devices  388 us (85%)
  matrix products  32.6 us (7%)
  between operations  14.2 us (3%)
  local copies, waits for them, and re-layouts  8.6 us (2%)
  other arithmetic  7.35 us (2%)
    reduce_scatter x1, waiting for transfers between devices, per_device(): lax.psum_scatter(jnp.concatenate([jnp.dot(block, gate_weight, preferred_e...  100 us
    reduce_scatter x1, waiting for transfers between devices, per_device(): lax.psum_scatter(times_transposed(block, down_weight).astype(jnp.bfloat16...  79 us
    psum x1, waiting for transfers between devices, per_device(): output = lax.psum(output_part.astype(jnp.bfloat16), 'col')  57.7 us
    all_gather x1, waiting for transfers between devices, per_device(): hidden_all = lax.all_gather(activate(gate, up), 'row', axis=0, tiled=True)  52.2 us
    all_gather x1, waiting for transfers between devices, per_device(): lax.all_gather(gate_pre, 'row', axis=0, tiled=True)  49.1 us
    all_gather x1, waiting for transfers between devices, per_device(): lax.all_gather(up_pre, 'row', axis=0, tiled=True)  48.9 us
    dot_general x3, matrix products, times_transposed(): lax.dot_general(left, right, (((1,), (1,)), ((), ())), preferred_element_...  12.5 us
    dot_general x3, matrix products, transposed_times(): lax.dot_general(left, right, (((0,), (0,)), ((), ())), preferred_element_...  10.7 us
  transfers between devices with their start and end apart: 6, of which 6 were waited for; matrix products, arithmetic and copies ran while one was open for 7% of the time, Pallas kernels for 0%

commit v1 on v0

v1 whole, which is shorter than its diff:
```python
import functools

import jax
import jax.numpy as jnp
from jax import lax
from jax.experimental import pallas as pl
from jax.experimental.pallas import tpu as pltpu
from jax.sharding import PartitionSpec as P

MESH = pl.DeviceIdType.MESH
BF, F32 = jnp.bfloat16, jnp.float32
CHUNKS, RING, ROWS, N_Z = 4, 4, 16, 8
BLOCK = RING * RING * ROWS
WIDTH, HALF = 256, 896
COLS = 3 * HALF
SPLIT = 1408
N_SEMS = 48

ORDER = [
    (0, 0), (0, 1), (1, 0), (2, 0), (1, 1), (3, 0), (0, 2), (4, 0), (2, 1), (5, 0), (3, 1), (1, 2), (6, 0),
    (4, 1), (0, 3), (2, 2), (5, 1), (7, 0), (3, 2), (6, 1), (1, 3), (8, 0), (4, 2), (2, 3), (5, 2), (7, 1),
    (3, 3), (9, 0), (6, 2), (8, 1), (4, 3), (10, 0), (5, 3), (7, 2), (9, 1), (6, 3), (11, 0), (8, 2), (10, 1), (7, 3), (9, 2),
    (11, 1), (8, 3), (10, 2), (9, 3),
]


def dot(left, right):
    return jnp.dot(left, right, preferred_element_type=F32)


def dot_t(left, right):
    return lax.dot_general(left, right, (((1,), (1,)), ((), ())), preferred_element_type=F32)


def kernel(
    tok_in, gw_in, uw_in, dw_in, cot_in,
    out, tok_grad, gate_grad, up_grad, down_grad,
    tok, cot, tok_p, cot_p, gu, gu_p, dw, dw_p, tok_t, cot_t,
    part, rec_a, rec_b, rec_l, rec_r, summed, sec_a, sec_b, sec_l, sec_r,
    own, other, z_part, z_rec, z_sum, grads, grads_d,
    send, recv, swap_send, swap_recv, local,
):
    row, z = lax.axis_index("row"), lax.axis_index("col")
    y, x, core = row // 8, (row // 2) % 4, row % 2
    a = x + core * (y - x)
    b = y + core * (x - y)

    def step_a(by):
        return (
            ((y + core * by + 4) % 4) * 8 + ((x + (1 - core) * by + 4) % 4) * 2 + core,
            z,
        )

    def step_b(by):
        return (
            ((y + (1 - core) * by + 4) % 4) * 8 + ((x + core * by + 4) % 4) * 2 + core,
            z,
        )

    a_next, a_prev, b_next, b_prev = step_a(1), step_a(-1), step_b(1), step_b(-1)
    partner = (y * 8 + x * 2 + 1 - core, z)
    others = [(row, (z + j) % N_Z) for j in range(1, N_Z)]
    a1, a2, a3 = (a + 1) % 4, (a + 2) % 4, (a + 3) % 4
    b1, b2, b3 = (b + 1) % 4, (b + 2) % 4, (b + 3) % 4
    left, right = pl.ds(0, SPLIT), pl.ds(SPLIT, COLS - SPLIT)
    mine = pl.multiple_of(core * HALF, 128)
    theirs = pl.multiple_of((1 - core) * HALF, 128)

    loads = [
        (gw_in.at[:, pl.ds(h * HALF, HALF)], gu.at[h, :, pl.ds(0, HALF)]) for h in range(2)
    ] + [
        (uw_in.at[:, pl.ds(h * HALF, HALF)], gu.at[h, :, pl.ds(HALF, HALF)]) for h in range(2)
    ] + [(dw_in, dw)]
    loads = [pltpu.make_async_copy(s, d, local.at[i]) for i, (s, d) in enumerate(loads)]

    @pl.when(core == 0)
    def _():
        pltpu.make_async_copy(tok_in, tok, local.at[5]).start()
        pltpu.make_async_copy(cot_in, cot, local.at[6]).start()

    @pl.when(core == 1)
    def _():
        for k in range(4):
            pltpu.make_async_copy(tok_in.at[:, :, k], tok.at[:, k], local.at[5]).start()
        for k in range(4):
            pltpu.make_async_copy(cot_in.at[:, :, k], cot.at[:, k], local.at[6]).start()

    for load in loads:
        load.start()

    barrier = pltpu.get_barrier_semaphore()
    peers = [partner, a_next, a_prev, b_next, b_prev] + others
    for peer in peers:
        pl.semaphore_signal(barrier, inc=1, device_id=peer, device_id_type=MESH)
    pl.semaphore_wait(barrier, len(peers))

    def remote(src, dst, s, r, to):
        return pltpu.make_async_remote_copy(
            src_ref=src, dst_ref=dst, send_sem=s, recv_sem=r, device_id=to, device_id_type=MESH
        )

    def swap(src, dst, i):
        return remote(src, dst, swap_send.at[i], swap_recv.at[i], partner)

    swaps = [
        swap(tok_in, tok_p, 0),
        swap(gw_in.at[:, pl.ds(theirs, HALF)], gu_p.at[:, pl.ds(0, HALF)], 1),
        swap(uw_in.at[:, pl.ds(theirs, HALF)], gu_p.at[:, pl.ds(HALF, HALF)], 2),
        swap(cot_in, cot_p, 3),
        swap(dw_in.at[1 - core], dw_p, 4),
    ]

    def swap_rows(src, dst, i):
        @pl.when(core == 1)
        def _():
            swap(src, dst, i).start()

        @pl.when(core == 0)
        def _():
            for k in range(4):
                swap(src.at[:, :, k], dst.at[:, k], i).start()

    swap_rows(tok_in, tok_p, 0)
    swaps[1].start()
    swaps[2].start()
    swap_rows(cot_in, cot_p, 3)
    swaps[4].start()

    pltpu.make_async_copy(tok_in, tok, local.at[5]).wait()
    pltpu.make_async_copy(cot_in, cot, local.at[6]).wait()
    for load in loads:
        load.wait()

    sent = []
    flows = {}

    def start(r, name, src, dst, to):
        i = len([key for key in flows if key[0] == r])
        copy = remote(src, dst, send.at[r, i], recv.at[r, i], to)
        flows[r, name] = copy
        copy.start()

    def arrived(r, *names):
        for name in names:
            flows[r, name].wait_recv()

    def flat(value):
        return value.reshape((BLOCK, value.shape[-1]))

    def project(r):
        t, tp = flat(tok[r]), flat(tok_p[r])
        for n in range(7):
            cols = pl.ds(n * 256, 256)
            total = dot(t, gu[core, :, cols]) + dot(tp, gu_p[:, cols])
            part[r, :, :, :, cols] = total.astype(BF).reshape((RING, RING, ROWS, 256))
        c, cp = flat(cot[r]), flat(cot_p[r])
        for n in range(0, HALF, 256):
            size = min(256, HALF - n)
            units = pl.ds(n, size)
            total = dot_t(c, dw[core, units, :]) + dot_t(cp, dw_p[units, :])
            part[r, :, :, :, pl.ds(2 * HALF + n, size)] = total.astype(BF).reshape((RING, RING, ROWS, size))

    def add(blocks, into, terms, begin, size):
        def step(i, carry):
            for n in range(begin, begin + size, 640 if size % 640 == 0 else 128 * 11 if size == SPLIT else 896):
                width = 640 if size % 640 == 0 else 128 * 11 if size == SPLIT else 896
                cols = pl.ds(n, width)
                total = terms[0](i, cols).astype(F32)
                for term in terms[1:]:
                    total = total + term(i, cols).astype(F32)
                into(i, cols, total.astype(BF))
            return carry

        lax.fori_loop(0, blocks, step, 0)

    def stage0(r):
        if r == 0:
            for copy in swaps:
                copy.wait_recv()
        project(r)
        start(r, "a1+", part.at[r, a2, :, :, left], rec_a.at[r], a_next)
        start(r, "a1-", part.at[r, a2, :, :, right], rec_b.at[r], a_prev)
        start(r, "a2+R", part.at[r, a1, :, :, right], rec_l.at[r, :, :, right], a_next)
        start(r, "a2-L", part.at[r, a3, :, :, left], rec_r.at[r, :, :, left], a_prev)

    def put_part(r, k):
        def put(i, cols, value):
            part[r, k, i, :, cols] = value
        return put

    def stage1(r):
        arrived(r, "a1+", "a1-")
        add(4, put_part(r, a1), [lambda i, cols: part[r, a1, i, :, cols], lambda i, cols: rec_a[r, i, :, cols]], 0, SPLIT)
        start(r, "a2+L", part.at[r, a1, :, :, left], rec_l.at[r, :, :, left], a_next)
        add(
            4, put_part(r, a3),
            [
                lambda i, cols: part[r, a3, i, :, cols],
                lambda i, cols: rec_b[r, i, :, pl.ds(cols.start - SPLIT, cols.size)],
            ],
            SPLIT, COLS - SPLIT,
        )
        start(r, "a2-R", part.at[r, a3, :, :, right], rec_r.at[r, :, :, right], a_prev)

    def stage2(r):
        arrived(r, "a2+R", "a2-L", "a2+L", "a2-R")

        def put(i, cols, value):
            summed[r, i, :, cols] = value

        add(
            4, put,
            [
                lambda i, cols: part[r, a, i, :, cols],
                lambda i, cols: rec_l[r, i, :, cols],
                lambda i, cols: rec_r[r, i, :, cols],
            ],
            0, COLS,
        )
        start(r, "b1+", summed.at[r, b2, :, left], sec_a.at[r], b_next)
        start(r, "b1-", summed.at[r, b2, :, right], sec_b.at[r], b_prev)
        start(r, "b2+R", summed.at[r, b1, :, right], sec_l.at[r, :, right], b_next)
        start(r, "b2-L", summed.at[r, b3, :, left], sec_r.at[r, :, left], b_prev)

    def stage3(r):
        arrived(r, "b1+", "b1-")
        value = summed[r, b1, :, left].astype(F32) + sec_a[r].astype(F32)
        summed[r, b1, :, left] = value.astype(BF)
        start(r, "b2+L", summed.at[r, b1, :, left], sec_l.at[r, :, left], b_next)
        value = summed[r, b3, :, right].astype(F32) + sec_b[r].astype(F32)
        summed[r, b3, :, right] = value.astype(BF)
        start(r, "b2-R", summed.at[r, b3, :, right], sec_r.at[r, :, right], b_prev)

    def stage4(r):
        arrived(r, "b2+R", "b2-L", "b2+L", "b2-R")

        def total(k):
            cols = pl.ds(k * HALF, HALF)
            value = summed[r, b, :, cols].astype(F32) + sec_l[r, :, cols].astype(F32) + sec_r[r, :, cols].astype(F32)
            return value.astype(BF).astype(F32)

        gate, up, grad = total(0), total(1), total(2)
        sig = jax.nn.sigmoid(gate)
        own[r, a, b, :, pl.ds(0, HALF)] = (gate * sig * up).astype(BF)
        own[r, a, b, :, pl.ds(HALF, HALF)] = (grad * up * sig * (1.0 + gate * (1.0 - sig))).astype(BF)
        own[r, a, b, :, pl.ds(2 * HALF, HALF)] = (grad * gate * sig).astype(BF)
        start(r, "c1+", own.at[r, a, b], own.at[r, a, b], b_next)
        start(r, "c1-", own.at[r, a, b], own.at[r, a, b], b_prev)

    def stage5(r):
        arrived(r, "c1+", "c1-")
        start(r, "c2+", own.at[r, a, b3, :, left], own.at[r, a, b3, :, left], b_next)
        start(r, "c2-", own.at[r, a, b1, :, right], own.at[r, a, b1, :, right], b_prev)

    def share(r, name, k):
        start(r, name, own.at[r, k], other.at[r, :, k], partner)

    def stage6(r):
        arrived(r, "c2+", "c2-")
        start(r, "d1+", own.at[r, a], own.at[r, a], a_next)
        start(r, "d1-", own.at[r, a], own.at[r, a], a_prev)
        share(r, "s0", a)

    def stage7(r):
        arrived(r, "d1+", "d1-")
        start(r, "d2+", own.at[r, a3, :, :, left], own.at[r, a3, :, :, left], a_next)
        start(r, "d2-", own.at[r, a1, :, :, right], own.at[r, a1, :, :, right], a_prev)
        share(r, "s1", a1)
        share(r, "s3", a3)

    def stage8(r):
        arrived(r, "d2+", "d2-")
        share(r, "s2", a2)

    def stage9(r):
        arrived(r, "s0", "s1", "s3", "s2")
        hidden, pre = pl.ds(0, HALF), pl.ds(HALF, 2 * HALF)
        total = dot(flat(own[r, :, :, :, hidden]), dw[core]) + dot(flat(other[r, :, :, :, hidden]), dw[1 - core])
        z_part[r, :, :, pl.ds(0, WIDTH)] = total.astype(BF).reshape((RING * RING, ROWS, WIDTH))
        total = dot_t(flat(own[r, :, :, :, pre]), gu[core]) + dot_t(flat(other[r, :, :, :, pre]), gu[1 - core])
        z_part[r, :, :, pl.ds(WIDTH, WIDTH)] = total.astype(BF).reshape((RING * RING, ROWS, WIDTH))
        for j in (4, 3, 5, 2, 6, 1, 7):
            target = (z + j) % N_Z
            start(r, f"e{j}", z_part.at[r, pl.ds(target * 2, 2)], z_rec.at[r, j - 1], others[j - 1])

    def stage10(r):
        arrived(r, *[f"e{j}" for j in range(1, N_Z)])
        total = z_part[r, pl.ds(z * 2, 2)].astype(F32)
        for j in range(N_Z - 1):
            total = total + z_rec[r, j].astype(F32)
        here = z_sum.at[r, pl.ds(z * 2, 2)]
        z_sum[r, pl.ds(z * 2, 2)] = total.astype(BF)
        for j in (4, 3, 5, 2, 6, 1, 7):
            start(r, f"f{j}", here, here, others[j - 1])

    def stores(r):
        result = []
        for k in range(4):
            for n, array in enumerate((out, tok_grad)):
                result.append((k, n, array))
        return result

    def stage11(r):
        arrived(r, *[f"f{j}" for j in range(1, N_Z)])

        @pl.when(core == 0)
        def _():
            for k in range(4):
                for n, array in enumerate((out, tok_grad)):
                    pltpu.make_async_copy(
                        z_sum.at[r, pl.ds(4 * k, 4), :, pl.ds(n * WIDTH, WIDTH)], array.at[r, k], local.at[7 + n]
                    ).start()

        @pl.when(core == 1)
        def _():
            for k in range(4):
                for n, array in enumerate((out, tok_grad)):
                    pltpu.make_async_copy(
                        z_sum.at[r, pl.ds(4 * k, 4), :, pl.ds(n * WIDTH, WIDTH)], array.at[r, :, k], local.at[7 + n]
                    ).start()

    def weight_grads(k, half, held):
        t, c = tok_t[...], cot_t[...]

        def tall(cols):
            return held[:, :, :, :, cols].reshape((CHUNKS * BLOCK, cols.size))

        for n in range(7):
            grads[k, :, pl.ds(n * 256, 256)] = dot(t, tall(pl.ds(HALF + n * 256, 256))).astype(BF)
        for n in range(0, HALF, 256):
            size = min(256, HALF - n)
            grads_d[k, pl.ds(n, size), :] = dot(c, tall(pl.ds(n, size))).T.astype(BF)
        cols = pl.ds(pl.multiple_of(half * HALF, 128), HALF)
        copies = [
            pltpu.make_async_copy(grads.at[k, :, pl.ds(0, HALF)], gate_grad.at[:, cols], local.at[9 + 3 * k]),
            pltpu.make_async_copy(grads.at[k, :, pl.ds(HALF, HALF)], up_grad.at[:, cols], local.at[10 + 3 * k]),
            pltpu.make_async_copy(grads_d.at[k], down_grad.at[half], local.at[11 + 3 * k]),
        ]
        for copy in copies:
            copy.start()
        return copies

    stages = [
        stage0, stage1, stage2, stage3, stage4, stage5, stage6, stage7, stage8, stage9, stage10, stage11,
    ]
    for i, (stage, r) in enumerate(ORDER):
        stages[stage](r)
        if i == 2:
            tok_t[...] = tok[...].reshape((CHUNKS * BLOCK, WIDTH)).T
            cot_t[...] = cot[...].reshape((CHUNKS * BLOCK, WIDTH)).T
    copies = weight_grads(0, core, own)
    stage10(3)
    copies += weight_grads(1, 1 - core, other)
    stage11(2)
    stage11(3)
    for copy in swaps:
        copy.wait_send()
    for copy in flows.values():
        copy.wait_send()
    pltpu.make_async_copy(out, out, local.at[7]).wait()
    pltpu.make_async_copy(tok_grad, tok_grad, local.at[8]).wait()
    for copy in copies:
        copy.wait()


def per_device(tokens, gate_weight, up_weight, down_weight, cotangent):
    rows = (CHUNKS, RING, RING, ROWS, WIDTH)
    grad = (CHUNKS, RING, RING, ROWS)
    V = pltpu.VMEM
    wide = (CHUNKS, RING, ROWS, COLS)
    any_space = pl.BlockSpec(memory_space=pl.ANY)
    S = jax.ShapeDtypeStruct
    outs = pl.pallas_call(
        kernel,
        out_shape=(
            S(rows, BF), S(rows, BF), S((WIDTH, 2 * HALF), BF), S((WIDTH, 2 * HALF), BF), S((2, HALF, WIDTH), BF),
        ),
        in_specs=[any_space] * 5,
        out_specs=[any_space] * 5,
        scratch_shapes=[
            V(rows, BF), V(rows, BF), V(rows, BF), V(rows, BF),
            V((2, WIDTH, 2 * HALF), BF), V((WIDTH, 2 * HALF), BF),
            V((2, HALF, WIDTH), BF), V((HALF, WIDTH), BF),
            V((WIDTH, CHUNKS * BLOCK), BF), V((WIDTH, CHUNKS * BLOCK), BF),
            V(grad + (COLS,), BF),
            V((CHUNKS, RING, ROWS, SPLIT), BF), V((CHUNKS, RING, ROWS, COLS - SPLIT), BF),
            V(wide, BF), V(wide, BF), V(wide, BF),
            V((CHUNKS, ROWS, SPLIT), BF), V((CHUNKS, ROWS, COLS - SPLIT), BF),
            V((CHUNKS, ROWS, COLS), BF), V((CHUNKS, ROWS, COLS), BF),
            V(grad + (COLS,), BF), V(grad + (COLS,), BF),
            V((CHUNKS, RING * RING, ROWS, 2 * WIDTH), BF),
            V((CHUNKS, N_Z - 1, 2, ROWS, 2 * WIDTH), BF),
            V((CHUNKS, RING * RING, ROWS, 2 * WIDTH), BF),
            V((2, WIDTH, 2 * HALF), BF), V((2, HALF, WIDTH), BF),
            pltpu.SemaphoreType.DMA((CHUNKS, N_SEMS)), pltpu.SemaphoreType.DMA((CHUNKS, N_SEMS)),
            pltpu.SemaphoreType.DMA((5,)), pltpu.SemaphoreType.DMA((5,)),
            pltpu.SemaphoreType.DMA((15,)),
        ],
        compiler_params=pltpu.CompilerParams(
            collective_id=0, has_side_effects=True, vmem_limit_bytes=58 << 20
        ),
    )(
        tokens.reshape(rows), gate_weight, up_weight, down_weight.reshape((2, HALF, WIDTH)), cotangent.reshape(rows),
    )
    output, tokens_grad, gate_grad, up_grad, down_grad = outs
    return (
        output.reshape(tokens.shape), tokens_grad.reshape(tokens.shape), gate_grad, up_grad,
        down_grad.reshape(down_weight.shape),
    )


def solution(mesh):
    return jax.shard_map(
        per_device,
        mesh=mesh,
        in_specs=(
            P(None, "row"),
            P("row", "col"),
            P("row", "col"),
            P("col", "row"),
            P(None, "row"),
        ),
        out_specs=(
            P(None, "row"),
            P(None, "row"),
            P("row", "col"),
            P("row", "col"),
            P("col", "row"),
        ),
        check_vma=False,
    )
```

time: 455 us -> 131 us (0.29)
  the two profiles are of different devices: /device:TPU:1 before, /device:TPU:10 now
where the time goes in v1:
time: 131 us
  Pallas kernels  124 us (95%)
  local copies, waits for them, and re-layouts  6.72 us (5%)
    pallas_call x1, Pallas kernels, per_device(): pl.pallas_call(kernel, out_shape=(S(rows, BF), S(rows, BF), S((WIDTH, 2 *...  124 us
    unnamed x13, local copies, waits for them, and re-layouts  6.72 us

profile of v1, /device:TPU:10, one launch (start us, length us, event | category | flops | bytes accessed | tf_op | source)
XLA Modules:
  0.0 131.3 jit_solution(3076685466421844047)
XLA Ops:
  0.6 123.9 %shard_map.92 = (bf16[4,4,4,16,256]{4,3,2,1,0:T(8,128)(2,1)}, bf16[4,4,4,16,256]{4,3,2,1,0:T(8,128)(2,1)}, bf16[256,1792]{1,0:T(8,128)(2,1)}, bf16[256,1792]{1,0:T(8,128)(2,1)}, bf16[2,896,256]{2,1,0:T(8,128)(2,1)}) custom-call(bf16[4,4,4,16,256]{4,3,2,1,0:T(8,128)(2,1)} %bitcast.10, bf16[256,1792]{1,0:T(8,128)(2,1)} %gw_in.1, bf16[256,1792]{1,0:T(8,128)(2,1)} %uw_in.1, ...), custom_call_target="tpu_custom_call" | custom-call | tf_op jit(solution)/shard_map/pallas_call | solution.py:373
  124.5 0.0 copy-start.3
  124.5 0.0 copy-start.2
  124.6 2.0 %copy.15 = bf16[1024,256]{1,0:T(8,128)(2,1)} copy(bf16[1024,256]{1,0:T(8,128)(2,1)} %bitcast.9) | data formatting | bytes 1048576
  126.5 0.0 copy-done.3
  126.5 0.8 copy.16
  127.3 0.0 copy-done.2
  127.3 0.0 copy-start.1
  127.3 0.9 copy.17
  128.3 0.6 copy-done.1
  128.8 0.0 copy-start
  128.8 0.9 copy.18
  129.8 0.6 copy-done
  130.4 0.9 copy.19
Async XLA Ops:
  124.5 2.0 %copy-start.3 = (bf16[4,4,4,16,256]{4,3,2,1,0:T(8,128)(2,1)S(1)}, bf16[4,4,4,16,256]{4,3,2,1,0:T(8,128)(2,1)}, u32[]{:S(2)}) copy-start(bf16[4,4,4,16,256]{4,3,2,1,0:T(8,128)(2,1)} %get-tuple-element.11) | copy-start | bytes 1572868
  124.5 2.8 %copy-start.2 = (bf16[256,1792]{1,0:T(8,128)(2,1)S(1)}, bf16[256,1792]{1,0:T(8,128)(2,1)}, u32[]{:S(2)}) copy-start(bf16[256,1792]{1,0:T(8,128)(2,1)} %get-tuple-element.22) | copy-start | bytes 2752516
  127.3 1.5 %copy-start.1 = (bf16[256,1792]{1,0:T(8,128)(2,1)S(1)}, bf16[256,1792]{1,0:T(8,128)(2,1)}, u32[]{:S(2)}) copy-start(bf16[256,1792]{1,0:T(8,128)(2,1)} %get-tuple-element.23) | copy-start | bytes 2752516
  128.8 1.5 %copy-start = (bf16[2,896,256]{2,1,0:T(8,128)(2,1)S(1)}, bf16[2,896,256]{2,1,0:T(8,128)(2,1)}, u32[]{:S(2)}) copy-start(bf16[2,896,256]{2,1,0:T(8,128)(2,1)} %get-tuple-element.14) | copy-start | bytes 2752516

commit v2 on v0

v2 whole, which is shorter than its diff:
```python
import functools

import jax
import jax.numpy as jnp
from jax import lax
from jax.experimental import pallas as pl
from jax.experimental.pallas import tpu as pltpu
from jax.sharding import PartitionSpec as P

MESH = pl.DeviceIdType.MESH
BF, F32 = jnp.bfloat16, jnp.float32
CHUNKS, RING, ROWS, N_Z = 4, 4, 16, 8
BLOCK = RING * RING * ROWS
WIDTH, HALF = 256, 896
N_SEMS = 40
TREE = {(0, 1), (2, 1), (0, 0), (1, 1), (2, 0), (3, 0), (1, 0)}
Z_PEERS = (1, 2, 3, 4, 5, 6, 7)
RS_LEFT, RS_RIGHT = (pl.ds(0, 896), pl.ds(0, 512)), (pl.ds(896, 896), pl.ds(512, 384))
AG_LEFT, AG_RIGHT = (pl.ds(0, 512), pl.ds(0, 896)), (pl.ds(512, 384), pl.ds(896, 896))

ORDER = [
    (0, 0, 0), (0, 0, 1), (14, 0, 0), (0, 1, 0), (1, 0, 0), (1, 0, 1), (0, 1, 1), (1, 1, 0),
    (0, 2, 0), (2, 0, 0), (2, 0, 1), (1, 1, 1), (2, 1, 0), (0, 2, 1), (1, 2, 0), (3, 0, 0),
    (3, 0, 1), (0, 3, 0), (3, 1, 0), (2, 1, 1), (1, 2, 1), (2, 2, 0), (4, 0, 0), (4, 0, 1),
    (1, 3, 0), (4, 1, 0), (3, 1, 1), (0, 3, 1), (2, 2, 1), (3, 2, 0), (5, 0, 0), (5, 0, 1),
    (2, 3, 0), (5, 1, 0), (4, 1, 1), (1, 3, 1), (3, 2, 1), (4, 2, 0), (6, 0, 0), (6, 0, 1),
    (3, 3, 0), (6, 1, 0), (5, 1, 1), (2, 3, 1), (4, 2, 1), (5, 2, 0), (7, 0, 0), (7, 0, 1),
    (4, 3, 0), (7, 1, 0), (6, 1, 1), (3, 3, 1), (5, 2, 1), (6, 2, 0), (8, 0, 0), (8, 0, 1),
    (9, 0, 0), (5, 3, 0), (8, 1, 0), (9, 0, 1), (9, 1, 0), (7, 1, 1), (4, 3, 1), (15, 0, 0),
    (6, 2, 1), (7, 2, 0), (15, 0, 1), (6, 3, 0), (15, 1, 0), (8, 1, 1), (10, 0, 0), (5, 3, 1),
    (9, 1, 1), (10, 0, 1), (10, 1, 0), (7, 2, 1), (8, 2, 0), (16, 0, 0), (7, 3, 0), (9, 2, 0),
    (6, 3, 1), (15, 1, 1), (16, 0, 1), (8, 2, 1), (16, 1, 0), (8, 3, 0), (9, 2, 1), (11, 0, 0),
    (9, 3, 0), (15, 2, 0), (12, 0, 0), (7, 3, 1), (10, 1, 1), (11, 0, 1), (11, 1, 0), (12, 1, 0),
    (15, 2, 1), (15, 3, 0), (8, 3, 1), (10, 2, 0), (16, 1, 1), (9, 3, 1), (10, 2, 1), (13, 0, 1),
    (10, 3, 0), (16, 2, 0), (11, 1, 1), (13, 1, 1), (10, 3, 1), (16, 2, 1), (16, 3, 0), (11, 2, 0),
    (11, 3, 1), (11, 2, 1), (11, 3, 0),]


def dot(left, right):
    return jnp.dot(left, right, preferred_element_type=F32)


def dot_t(left, right):
    return lax.dot_general(left, right, (((1,), (1,)), ((), ())), preferred_element_type=F32)


def kernel(
    tok_in, gw_in, uw_in, dw_in, cot_in,
    z_sum, grads, grads_d,
    tok, cot, tok_p, cot_p, gu, gu_p, dw, dw_p, tok_t, cot_t,
    part, rec_a, rec_b, rec_l, rec_r, summed, sec_a, sec_b, sec_l, sec_r,
    acts, own, other, z_part, z_rec,
    send, recv, swap_send, swap_recv, local,
):
    row, z = lax.axis_index("row"), lax.axis_index("col")
    y, x, core = row // 8, (row // 2) % 4, row % 2
    a = x + core * (y - x)
    b = y + core * (x - y)

    def step_a(by):
        return (
            ((y + core * by + 4) % 4) * 8 + ((x + (1 - core) * by + 4) % 4) * 2 + core,
            z,
        )

    def step_b(by):
        return (
            ((y + (1 - core) * by + 4) % 4) * 8 + ((x + core * by + 4) % 4) * 2 + core,
            z,
        )

    a_next, a_prev, b_next, b_prev = step_a(1), step_a(-1), step_b(1), step_b(-1)
    partner = (y * 8 + x * 2 + 1 - core, z)
    others = [(row, (z + j) % N_Z) for j in range(1, N_Z)]
    a1, a2, a3 = (a + 1) % 4, (a + 2) % 4, (a + 3) % 4
    b1, b2, b3 = (b + 1) % 4, (b + 2) % 4, (b + 3) % 4
    theirs = pl.multiple_of((1 - core) * HALF, 128)

    waits = {}

    def rows_of(ref, first, count):
        return ref.at[pl.ds(first, count)]

    def load(name, src, dst):
        i = len(waits)
        copy = pltpu.make_async_copy(src, dst, local.at[i])
        waits[name] = copy.wait
        copy.start()

    def load_rows(name, src, dst, first, count):
        sem = local.at[len(waits)]
        waits[name] = pltpu.make_async_copy(rows_of(src, first, count), rows_of(dst, first, count), sem).wait

        @pl.when(core == 0)
        def _():
            pltpu.make_async_copy(rows_of(src, first, count), rows_of(dst, first, count), sem).start()

        @pl.when(core == 1)
        def _():
            for k in range(4):
                pltpu.make_async_copy(
                    src.at[pl.ds(first, count), :, k], dst.at[pl.ds(first, count), k], sem
                ).start()

    def use(*names):
        for name in names:
            if name in waits:
                waits.pop(name)()

    def load_weights(name, half):
        cols = pl.ds(pl.multiple_of(half * HALF, 128), HALF)
        load(name + "_gate", gw_in.at[:, cols], gu.at[half, :, pl.ds(0, HALF)])
        load(name + "_up", uw_in.at[:, cols], gu.at[half, :, pl.ds(HALF, HALF)])
        load(name + "_down", dw_in.at[half], dw.at[half])

    load_rows("tok0", tok_in, tok, 0, 1)
    load_weights("mine", core)
    load_rows("cot0", cot_in, cot, 0, 1)

    barrier = pltpu.get_barrier_semaphore()
    peers = [partner, a_next, a_prev, b_next, b_prev] + [others[j - 1] for j in Z_PEERS]
    for peer in peers:
        pl.semaphore_signal(barrier, inc=1, device_id=peer, device_id_type=MESH)
    pl.semaphore_wait(barrier, len(peers))

    def remote(src, dst, s, r, to):
        return pltpu.make_async_remote_copy(
            src_ref=src, dst_ref=dst, send_sem=s, recv_sem=r, device_id=to, device_id_type=MESH
        )

    swaps = []

    def swap(name, src, dst):
        copy = remote(src, dst, swap_send.at[len(swaps)], swap_recv.at[len(swaps)], partner)
        swaps.append(copy)
        waits[name] = copy.wait_recv
        copy.start()

    def swap_rows(name, src, dst, first, count):
        i = len(swaps)

        def part_copy(src, dst):
            return remote(src, dst, swap_send.at[i], swap_recv.at[i], partner)

        whole = part_copy(rows_of(src, first, count), rows_of(dst, first, count))
        swaps.append(whole)
        waits[name] = whole.wait_recv

        @pl.when(core == 1)
        def _():
            whole.start()

        @pl.when(core == 0)
        def _():
            for k in range(4):
                part_copy(src.at[pl.ds(first, count), :, k], dst.at[pl.ds(first, count), k]).start()

    swap_rows("tok_p0", tok_in, tok_p, 0, 1)
    swap("gate_p", gw_in.at[:, pl.ds(theirs, HALF)], gu_p.at[:, pl.ds(0, HALF)])
    swap("up_p", uw_in.at[:, pl.ds(theirs, HALF)], gu_p.at[:, pl.ds(HALF, HALF)])
    swap_rows("cot_p0", cot_in, cot_p, 0, 1)
    swap("down_p", dw_in.at[1 - core], dw_p)
    swap_rows("tok_p1", tok_in, tok_p, 1, CHUNKS - 1)
    swap_rows("cot_p1", cot_in, cot_p, 1, CHUNKS - 1)
    load_rows("tok1", tok_in, tok, 1, CHUNKS - 1)
    load_rows("cot1", cot_in, cot, 1, CHUNKS - 1)
    load_weights("theirs", 1 - core)

    flows = {}

    def start(unit, name, src, dst, to):
        r, g = unit
        i = len([key for key in flows if key[0] == unit])
        copy = remote(src, dst, send.at[2 * r + g, i], recv.at[2 * r + g, i], to)
        flows[unit, name] = copy
        copy.start()

    def arrived(unit, *names):
        for name in names:
            flows[unit, name].wait_recv()

    def flat(value):
        return value.reshape((BLOCK, value.shape[-1]))

    def add(blocks, begin, size, into, *terms):
        width = min(size, HALF)

        def step(i, carry):
            for n in range(begin, begin + size, width):
                total = terms[0](i, n, width).astype(F32)
                for term in terms[1:]:
                    total = total + term(i, n, width).astype(F32)
                into(i, n, width, total.astype(BF))
            return carry

        lax.fori_loop(0, blocks, step, 0)

    def stage0(unit):
        r, g = unit
        late = "" if r == 0 else "1"
        if g == 0:
            use("tok0", "mine_gate", "mine_up", "tok_p0", "gate_p", "up_p", "tok" + late, "tok_p" + late)
        else:
            use("cot0", "mine_down", "cot_p0", "down_p", "cot" + late, "cot_p" + late)
        dst = part[g]
        if g == 0:
            t, tp = flat(tok[r]), flat(tok_p[r])
            for n in range(0, 2 * HALF, 256):
                cols = pl.ds(n, 256)
                total = dot(t, gu[core, :, cols]) + dot(tp, gu_p[:, cols])
                dst[r, :, :, :, cols] = total.astype(BF).reshape((RING, RING, ROWS, 256))
        else:
            c, cp = flat(cot[r]), flat(cot_p[r])
            for n in range(0, HALF, 256):
                size = min(256, HALF - n)
                units = pl.ds(n, size)
                total = dot_t(c, dw[core, units, :]) + dot_t(cp, dw_p[units, :])
                dst[r, :, :, :, units] = total.astype(BF).reshape((RING, RING, ROWS, size))
        left, right = RS_LEFT[g], RS_RIGHT[g]
        start(unit, "a1+", dst.at[r, a2, :, :, left], rec_a[g].at[r], a_next)
        start(unit, "a1-", dst.at[r, a2, :, :, right], rec_b[g].at[r], a_prev)
        start(unit, "a2+R", dst.at[r, a1, :, :, right], rec_l[g].at[r, :, :, right], a_next)
        start(unit, "a2-L", dst.at[r, a3, :, :, left], rec_r[g].at[r, :, :, left], a_prev)

    def stage1(unit):
        r, g = unit
        left, right = RS_LEFT[g], RS_RIGHT[g]
        ref, from_a, from_b = part[g], rec_a[g], rec_b[g]
        arrived(unit, "a1+", "a1-")

        def put_left(i, n, width, value):
            ref[r, a1, i, :, pl.ds(n, width)] = value

        add(
            4, 0, left.size, put_left,
            lambda i, n, width: ref[r, a1, i, :, pl.ds(n, width)],
            lambda i, n, width: from_a[r, i, :, pl.ds(n, width)],
        )
        start(unit, "a2+L", ref.at[r, a1, :, :, left], rec_l[g].at[r, :, :, left], a_next)

        def put_right(i, n, width, value):
            ref[r, a3, i, :, pl.ds(n, width)] = value

        add(
            4, right.start, right.size, put_right,
            lambda i, n, width: ref[r, a3, i, :, pl.ds(n, width)],
            lambda i, n, width: from_b[r, i, :, pl.ds(n - right.start, width)],
        )
        start(unit, "a2-R", ref.at[r, a3, :, :, right], rec_r[g].at[r, :, :, right], a_prev)

    def stage2(unit):
        r, g = unit
        left, right = RS_LEFT[g], RS_RIGHT[g]
        ref, from_l, from_r, to = part[g], rec_l[g], rec_r[g], summed[g]
        arrived(unit, "a2+R", "a2-L", "a2+L", "a2-R")

        def put(i, n, width, value):
            to[r, i, :, pl.ds(n, width)] = value

        add(
            4, 0, left.size + right.size, put,
            lambda i, n, width: ref[r, a, i, :, pl.ds(n, width)],
            lambda i, n, width: from_l[r, i, :, pl.ds(n, width)],
            lambda i, n, width: from_r[r, i, :, pl.ds(n, width)],
        )
        start(unit, "b1+", to.at[r, b2, :, left], sec_a[g].at[r], b_next)
        start(unit, "b1-", to.at[r, b2, :, right], sec_b[g].at[r], b_prev)
        start(unit, "b2+R", to.at[r, b1, :, right], sec_l[g].at[r, :, right], b_next)
        start(unit, "b2-L", to.at[r, b3, :, left], sec_r[g].at[r, :, left], b_prev)

    def stage3(unit):
        r, g = unit
        left, right = RS_LEFT[g], RS_RIGHT[g]
        ref = summed[g]
        arrived(unit, "b1+", "b1-")
        value = ref[r, b1, :, left].astype(F32) + sec_a[g][r].astype(F32)
        ref[r, b1, :, left] = value.astype(BF)
        start(unit, "b2+L", ref.at[r, b1, :, left], sec_l[g].at[r, :, left], b_next)
        value = ref[r, b3, :, right].astype(F32) + sec_b[g][r].astype(F32)
        ref[r, b3, :, right] = value.astype(BF)
        start(unit, "b2-R", ref.at[r, b3, :, right], sec_r[g].at[r, :, right], b_prev)

    def stage4(unit):
        r, g = unit
        arrived(unit, "b2+R", "b2-L", "b2+L", "b2-R")

        def total(k):
            cols = pl.ds(k * HALF, HALF)
            value = summed[g][r, b, :, cols].astype(F32) + sec_l[g][r, :, cols].astype(F32)
            return (value + sec_r[g][r, :, cols].astype(F32)).astype(BF)

        low, high = pl.ds(0, HALF), pl.ds(HALF, HALF)
        if g == 0:
            gate_bf, up_bf = total(0), total(1)
            acts[r, :, low] = gate_bf
            acts[r, :, high] = up_bf
            gate, up = gate_bf.astype(F32), up_bf.astype(F32)
            own[0][r, a, b] = (gate * jax.nn.sigmoid(gate) * up).astype(BF)
        else:
            gate, up, grad = acts[r, :, low].astype(F32), acts[r, :, high].astype(F32), total(0).astype(F32)
            sig = jax.nn.sigmoid(gate)
            own[1][r, a, b, :, low] = (grad * up * sig * (1.0 + gate * (1.0 - sig))).astype(BF)
            own[1][r, a, b, :, high] = (grad * gate * sig).astype(BF)
        start(unit, "c1+", own[g].at[r, a, b], own[g].at[r, a, b], b_next)
        start(unit, "c1-", own[g].at[r, a, b], own[g].at[r, a, b], b_prev)

    def stage5(unit):
        r, g = unit
        left, right = AG_LEFT[g], AG_RIGHT[g]
        arrived(unit, "c1+", "c1-")
        start(unit, "c2+", own[g].at[r, a, b3, :, left], own[g].at[r, a, b3, :, left], b_next)
        start(unit, "c2-", own[g].at[r, a, b1, :, right], own[g].at[r, a, b1, :, right], b_prev)

    def share(unit, name, k):
        r, g = unit
        start(unit, name, own[g].at[r, k], other[g].at[r, :, k], partner)

    def stage6(unit):
        r, g = unit
        arrived(unit, "c2+", "c2-")
        start(unit, "d1+", own[g].at[r, a], own[g].at[r, a], a_next)
        start(unit, "d1-", own[g].at[r, a], own[g].at[r, a], a_prev)
        share(unit, "s0", a)

    def stage7(unit):
        r, g = unit
        left, right = AG_LEFT[g], AG_RIGHT[g]
        arrived(unit, "d1+", "d1-")
        start(unit, "d2+", own[g].at[r, a3, :, :, left], own[g].at[r, a3, :, :, left], a_next)
        start(unit, "d2-", own[g].at[r, a1, :, :, right], own[g].at[r, a1, :, :, right], a_prev)
        share(unit, "s1", a1)
        share(unit, "s3", a3)

    def stage8(unit):
        arrived(unit, "d2+", "d2-")
        share(unit, "s2", a2)

    def stage9(unit):
        r, g = unit
        arrived(unit, "s0", "s1", "s3", "s2")
        ours, rest = flat(own[g][r]), flat(other[g][r])
        if g == 0:
            use("theirs_down")
            total = dot(ours, dw[core]) + dot(rest, dw[1 - core])
        else:
            use("theirs_gate", "theirs_up")
            total = dot_t(ours, gu[core]) + dot_t(rest, gu[1 - core])
        z_part[g, r] = total.astype(BF).reshape((RING, RING, ROWS, WIDTH))
        if unit not in TREE:
            for j in (4, 3, 5, 2, 6, 1, 7):
                start(unit, f"e{j}", piece(z_part, unit, j), z_rec.at[g, r, j - 1], others[j - 1])
            return
        start(unit, "e3", piece(z_part, unit, 5), z_rec.at[g, r, 2], others[6])
        start(unit, "e5", piece(z_part, unit, 3), z_rec.at[g, r, 3], others[0])
        start(unit, "e4a", piece(z_part, unit, 4).at[0], z_rec.at[g, r, 4, 0], others[5])
        start(unit, "e4b", piece(z_part, unit, 4).at[1], z_rec.at[g, r, 4, 1], others[1])
        start(unit, "e1", piece(z_part, unit, 1), z_rec.at[g, r, 0], others[0])
        start(unit, "e7", piece(z_part, unit, 7), z_rec.at[g, r, 1], others[6])

    def piece(ref, unit, by):
        r, g = unit
        target = (z + by) % N_Z
        return ref.at[g, r, target // 2, pl.ds((target % 2) * 2, 2)]

    def stage15(unit):
        r, g = unit
        arrived(unit, "e3", "e5", "e4a", "e4b")
        for by, slot, half in ((6, 2, 0), (2, 3, 1)):
            here = piece(z_part, unit, by)
            total = here[...].astype(F32) + z_rec[g, r, slot].astype(F32)
            both = [total[0], total[1]]
            both[half] = both[half] + z_rec[g, r, 4, half].astype(F32)
            here[0] = both[0].astype(BF)
            here[1] = both[1].astype(BF)
        start(unit, "e6", piece(z_part, unit, 6), z_rec.at[g, r, 5], others[5])
        start(unit, "e2", piece(z_part, unit, 2), z_rec.at[g, r, 6], others[1])

    def stage10(unit):
        r, g = unit
        tree = unit in TREE
        total = piece(z_part, unit, 0)[...].astype(F32)
        if tree:
            arrived(unit, "e1", "e7", "e2", "e6")
        else:
            arrived(unit, *[f"e{j}" for j in range(1, N_Z)])
        for j in (0, 1, 5, 6) if tree else range(N_Z - 1):
            total = total + z_rec[g, r, j].astype(F32)
        here = piece(z_sum, unit, 0)
        here[...] = total.astype(BF)
        for j in (2, 6, 1, 7) if tree else (4, 3, 5, 2, 6, 1, 7):
            start(unit, f"f{j}", here, here, others[j - 1])

    def stage16(unit):
        arrived(unit, "f2", "f6")
        far = piece(z_sum, unit, 6)
        start(unit, "f3", far, far, others[0])
        start(unit, "f4a", far.at[0], far.at[0], others[1])
        far = piece(z_sum, unit, 2)
        start(unit, "f5", far, far, others[6])
        start(unit, "f4b", far.at[1], far.at[1], others[5])

    def stage11(unit):
        if unit in TREE:
            arrived(unit, "f1", "f7", "f3", "f5", "f4a", "f4b")
        else:
            arrived(unit, *[f"f{j}" for j in range(1, N_Z)])

    def tall(held, cols):
        return held[:, :, :, :, cols].reshape((CHUNKS * BLOCK, cols.size))

    def stage12(unit):
        k = unit[0]
        held = (own, other)[k][0]
        c = cot_t[...]
        for n in range(0, HALF, 256):
            cols = pl.ds(n, min(256, HALF - n))
            grads_d[k, cols, :] = dot(c, tall(held, cols)).T.astype(BF)

    def stage13(unit):
        k = unit[0]
        held = (own, other)[k][1]
        t = tok_t[...]
        for n in range(7):
            cols = pl.ds(n * 256, 256)
            grads[k, :, cols] = dot(t, tall(held, cols)).astype(BF)

    def stage14(unit):
        use("tok0", "tok1", "cot0", "cot1")
        tok_t[...] = tok[...].reshape((CHUNKS * BLOCK, WIDTH)).T
        cot_t[...] = cot[...].reshape((CHUNKS * BLOCK, WIDTH)).T

    stages = [
        stage0, stage1, stage2, stage3, stage4, stage5, stage6, stage7, stage8, stage9, stage10, stage11,
        stage12, stage13, stage14, stage15, stage16,
    ]
    for i, r, g in ORDER:
        stages[i]((r, g))
    for copy in swaps:
        copy.wait_send()
    for copy in flows.values():
        copy.wait_send()
    use(*list(waits))


def write_out(z_sum, grads, grads_d, out, tok_grad, gate_grad, up_grad, down_grad, sems):
    core = lax.axis_index("row") % 2
    copies = []

    def copy(src, dst):
        copies.append(pltpu.make_async_copy(src, dst, sems.at[len(copies)]))

    for k, half in enumerate((core, 1 - core)):
        cols = pl.ds(pl.multiple_of(half * HALF, 128), HALF)
        copy(grads.at[k, :, pl.ds(0, HALF)], gate_grad.at[:, cols])
        copy(grads.at[k, :, pl.ds(HALF, HALF)], up_grad.at[:, cols])
        copy(grads_d.at[k], down_grad.at[half])
    for each in copies:
        each.start()
    for g, array in enumerate((out, tok_grad)):
        copy(z_sum.at[g], array)

        @pl.when(core == 0)
        def _():
            copies[-1].start()

        @pl.when(core == 1)
        def _():
            for k in range(4):
                pltpu.make_async_copy(z_sum.at[g, :, k], array.at[:, :, k], sems.at[len(copies) - 1]).start()

    for each in copies:
        each.wait()


def per_device(tokens, gate_weight, up_weight, down_weight, cotangent):
    rows = (CHUNKS, RING, RING, ROWS, WIDTH)
    grad = (CHUNKS, RING, RING, ROWS)
    V = pltpu.VMEM

    def pair(shape, cols):
        return tuple(V(shape + (n,), BF) for n in cols)

    S = jax.ShapeDtypeStruct
    hbm, vmem = pl.BlockSpec(memory_space=pltpu.HBM), pl.BlockSpec(memory_space=pltpu.VMEM)
    results = pl.pallas_call(
        kernel,
        out_shape=(V((2,) + rows, BF), V((2, WIDTH, 2 * HALF), BF), V((2, HALF, WIDTH), BF)),
        in_specs=[hbm] * 5,
        out_specs=[vmem] * 3,
        scratch_shapes=[
            V(rows, BF), V(rows, BF), V(rows, BF), V(rows, BF),
            V((2, WIDTH, 2 * HALF), BF), V((WIDTH, 2 * HALF), BF),
            V((2, HALF, WIDTH), BF), V((HALF, WIDTH), BF),
            V((WIDTH, CHUNKS * BLOCK), BF), V((WIDTH, CHUNKS * BLOCK), BF),
            pair(grad, (2 * HALF, HALF)),
            pair((CHUNKS, RING, ROWS), (896, 512)),
            pair((CHUNKS, RING, ROWS), (896, 384)),
            pair((CHUNKS, RING, ROWS), (2 * HALF, HALF)), pair((CHUNKS, RING, ROWS), (2 * HALF, HALF)),
            pair((CHUNKS, RING, ROWS), (2 * HALF, HALF)),
            pair((CHUNKS, ROWS), (896, 512)), pair((CHUNKS, ROWS), (896, 384)),
            pair((CHUNKS, ROWS), (2 * HALF, HALF)), pair((CHUNKS, ROWS), (2 * HALF, HALF)),
            V((CHUNKS, ROWS, 2 * HALF), BF),
            pair(grad, (HALF, 2 * HALF)), pair(grad, (HALF, 2 * HALF)),
            V((2,) + rows, BF),
            V((2, CHUNKS, N_Z - 1, 2, ROWS, WIDTH), BF),
            pltpu.SemaphoreType.DMA((2 * CHUNKS, N_SEMS)), pltpu.SemaphoreType.DMA((2 * CHUNKS, N_SEMS)),
            pltpu.SemaphoreType.DMA((8,)), pltpu.SemaphoreType.DMA((8,)),
            pltpu.SemaphoreType.DMA((24,)),
        ],
        compiler_params=pltpu.CompilerParams(
            collective_id=0, has_side_effects=True, vmem_limit_bytes=60 << 20
        ),
    )(
        tokens.reshape(rows), gate_weight, up_weight, down_weight.reshape((2, HALF, WIDTH)), cotangent.reshape(rows),
    )
    output, tokens_grad, gate_grad, up_grad, down_grad = pl.pallas_call(
        write_out,
        out_shape=(
            S(rows, BF), S(rows, BF), S((WIDTH, 2 * HALF), BF), S((WIDTH, 2 * HALF), BF), S((2, HALF, WIDTH), BF),
        ),
        in_specs=[vmem] * 3,
        out_specs=[hbm] * 5,
        scratch_shapes=[pltpu.SemaphoreType.DMA((8,))],
    )(*results)
    return (
        output.reshape(tokens.shape), tokens_grad.reshape(tokens.shape), gate_grad, up_grad,
        down_grad.reshape(down_weight.shape),
    )


def solution(mesh):
    return jax.shard_map(
        per_device,
        mesh=mesh,
        in_specs=(
            P(None, "row"),
            P("row", "col"),
            P("row", "col"),
            P("col", "row"),
            P(None, "row"),
        ),
        out_specs=(
            P(None, "row"),
            P(None, "row"),
            P("row", "col"),
            P("row", "col"),
            P("col", "row"),
        ),
        check_vma=False,
    )
```

time: 455 us -> 110 us (0.24)
  waiting for transfers between devices: 388 us -> 0 us
  Pallas kernels: 0 us -> 106 us
  matrix products: 32.6 us -> 0 us
  between operations: 14.2 us -> 0.81 us
  other arithmetic: 7.35 us -> 0 us
  local copies, waits for them, and re-layouts: 8.6 us -> 3.17 us
    reduce_scatter x2 -> x0, waiting for transfers between devices: 179 us -> none  [the longest x1 100 us: per_device(): lax.psum_scatter(jnp.concatenate([jnp.dot(block, gate_weight, preferred_e...]
    all_gather x3 -> x0, waiting for transfers between devices: 150 us -> none  [the longest x1 52.2 us: per_device(): hidden_all = lax.all_gather(activate(gate, up), 'row', axis=0, tiled=True)]
    pallas_call x0 -> x2, Pallas kernels: none -> 106 us  [the longest x1 102 us: per_device(): pl.pallas_call(kernel, out_shape=(V((2,) + rows, BF), V((2, WIDTH, 2 * HA...]
    psum x1 -> x0, waiting for transfers between devices: 57.7 us -> none  [per_device(): output = lax.psum(output_part.astype(jnp.bfloat16), 'col')]
    dot_general x9 -> x0, matrix products: 32.6 us -> none  [the longest x3 12.5 us: times_transposed(): lax.dot_general(left, right, (((1,), (1,)), ((), ())), preferred_element_...]
    concatenate x1 -> x0, other arithmetic: 5.5 us -> none  [per_device(): jnp.concatenate([jnp.dot(block, gate_weight, preferred_element_type=jnp.f...]
    unnamed x16 -> x6, local copies, waits for them, and re-layouts: 8.6 us -> 3.17 us
  transfers between devices with their start and end apart: 6 -> 0, of which waited for: 6 -> 0; matrix products, arithmetic and copies ran while one was open for 7% -> 0% of each run, Pallas kernels for 0% -> 0%
where the time goes in v2:
time: 110 us
  Pallas kernels  106 us (96%)
  local copies, waits for them, and re-layouts  3.17 us (3%)
    pallas_call x1, Pallas kernels, per_device(): pl.pallas_call(kernel, out_shape=(V((2,) + rows, BF), V((2, WIDTH, 2 * HA...  102 us
    pallas_call x1, Pallas kernels, per_device(): pl.pallas_call(write_out, out_shape=(S(rows, BF), S(rows, BF), S((WIDTH,...  3.97 us
    unnamed x6, local copies, waits for them, and re-layouts  3.17 us

profile of v2, /device:TPU:1, one launch (start us, length us, event | category | flops | bytes accessed | tf_op | source)
XLA Modules:
  0.0 109.9 jit_solution(18160090979645052452)
XLA Ops:
  0.6 101.9 %shard_map.92 = (bf16[2,4,4,4,16,256]{5,4,3,2,1,0:T(8,128)(2,1)S(1)}, bf16[2,256,1792]{2,1,0:T(8,128)(2,1)S(1)}, bf16[2,896,256]{2,1,0:T(8,128)(2,1)S(1)}) custom-call(bf16[4,4,4,16,256]{4,3,2,1,0:T(8,128)(2,1)} %bitcast.7, bf16[256,1792]{1,0:T(8,128)(2,1)} %gw_in.1, bf16[256,1792]{1,0:T(8,128)(2,1)} %uw_in.1, bf16[2,896,256]{2,1,0:T(8,128)(2,1)} %bitcast.6, ...), custom_call_target="tpu_custom_call" | custom-call | tf_op jit(solution)/shard_map/pallas_call | solution.py:485
  102.5 0.0 copy-start
  102.6 1.2 %copy-done = bf16[2,256,1792]{2,1,0:T(8,128)(2,1)} copy-done((bf16[2,256,1792]{2,1,0:T(8,128)(2,1)}, bf16[2,256,1792]{2,1,0:T(8,128)(2,1)S(1)}, u32[]{:S(2)}) %copy-start) | copy-done | bytes 1835032
  103.8 0.0 copy-start.1
  103.8 1.0 copy-done.1
  104.8 0.0 copy-start.2
  104.8 0.9 copy-done.2
  105.7 4.0 %shard_map.93 = (bf16[4,4,4,16,256]{4,3,2,1,0:T(8,128)(2,1)}, bf16[4,4,4,16,256]{4,3,2,1,0:T(8,128)(2,1)}, bf16[256,1792]{1,0:T(8,128)(2,1)}, bf16[256,1792]{1,0:T(8,128)(2,1)}, bf16[2,896,256]{2,1,0:T(8,128)(2,1)}) custom-call(bf16[2,4,4,4,16,256]{5,4,3,2,1,0:T(8,128)(2,1)} %copy-done.1, bf16[2,256,1792]{2,1,0:T(8,128)(2,1)} %copy-done, ...), custom_call_target="tpu_custom_call" | custom-call | tf_op jit(solution)/shard_map/pallas_call | solution.py:516
Async XLA Ops:
  102.5 1.3 %copy-start = (bf16[2,256,1792]{2,1,0:T(8,128)(2,1)}, bf16[2,256,1792]{2,1,0:T(8,128)(2,1)S(1)}, u32[]{:S(2)}) copy-start(bf16[2,256,1792]{2,1,0:T(8,128)(2,1)S(1)} %get-tuple-element.14.grads) | copy-start | bytes 5505028
  103.8 1.0 copy-start.1
  104.8 0.9 copy-start.2

commit v3 on v2

--- a/solution.py
+++ b/solution.py
@@ -1,4 +1,4 @@
-import functools
+import itertools
 
 import jax
 import jax.numpy as jnp
@@ -12,7 +12,8 @@
 CHUNKS, RING, ROWS, N_Z = 4, 4, 16, 8
 BLOCK = RING * RING * ROWS
 WIDTH, HALF = 256, 896
-N_SEMS = 40
+KINDS = ("a1", "a2", "b1", "b2", "c1", "c2", "d1", "d2", "s", "e1", "e2", "f1", "f2")
+SENDS = "efabcds"
 TREE = {(0, 1), (2, 1), (0, 0), (1, 1), (2, 0), (3, 0), (1, 0)}
 Z_PEERS = (1, 2, 3, 4, 5, 6, 7)
 RS_LEFT, RS_RIGHT = (pl.ds(0, 896), pl.ds(0, 512)), (pl.ds(896, 896), pl.ds(512, 384))
@@ -48,7 +49,7 @@
     tok_in, gw_in, uw_in, dw_in, cot_in,
     z_sum, grads, grads_d,
     tok, cot, tok_p, cot_p, gu, gu_p, dw, dw_p, tok_t, cot_t,
-    part, rec_a, rec_b, rec_l, rec_r, summed, sec_a, sec_b, sec_l, sec_r,
+    part, rec_in, rec_out, summed, sec_in, sec_out,
     acts, own, other, z_part, z_rec,
     send, recv, swap_send, swap_recv, local,
 ):
@@ -76,19 +77,18 @@
     b1, b2, b3 = (b + 1) % 4, (b + 2) % 4, (b + 3) % 4
     theirs = pl.multiple_of((1 - core) * HALF, 128)
 
-    waits = {}
+    waits, counter = {}, itertools.count()
 
     def rows_of(ref, first, count):
         return ref.at[pl.ds(first, count)]
 
     def load(name, src, dst):
-        i = len(waits)
-        copy = pltpu.make_async_copy(src, dst, local.at[i])
+        copy = pltpu.make_async_copy(src, dst, local.at[next(counter)])
         waits[name] = copy.wait
         copy.start()
 
     def load_rows(name, src, dst, first, count):
-        sem = local.at[len(waits)]
+        sem = local.at[next(counter)]
         waits[name] = pltpu.make_async_copy(rows_of(src, first, count), rows_of(dst, first, count), sem).wait
 
         @pl.when(core == 0)
@@ -166,18 +166,15 @@
     load_rows("cot1", cot_in, cot, 1, CHUNKS - 1)
     load_weights("theirs", 1 - core)
 
-    flows = {}
-
-    def start(unit, name, src, dst, to):
-        r, g = unit
-        i = len([key for key in flows if key[0] == unit])
-        copy = remote(src, dst, send.at[2 * r + g, i], recv.at[2 * r + g, i], to)
-        flows[unit, name] = copy
-        copy.start()
-
-    def arrived(unit, *names):
-        for name in names:
-            flows[unit, name].wait_recv()
+    def start(unit, kind, src, dst, to):
+        r, g = unit
+        place = SENDS.index(kind[0])
+        out_sem = place if place < 2 else 2 * place - 2 + g
+        remote(src, dst, send.at[out_sem], recv.at[KINDS.index(kind), 2 * r + g], to).start()
+
+    def arrived(unit, kind, ref):
+        r, g = unit
+        remote(ref, ref, send.at[0], recv.at[KINDS.index(kind), 2 * r + g], partner).wait_recv()
 
     def flat(value):
         return value.reshape((BLOCK, value.shape[-1]))
@@ -217,16 +214,16 @@
                 total = dot_t(c, dw[core, units, :]) + dot_t(cp, dw_p[units, :])
                 dst[r, :, :, :, units] = total.astype(BF).reshape((RING, RING, ROWS, size))
         left, right = RS_LEFT[g], RS_RIGHT[g]
-        start(unit, "a1+", dst.at[r, a2, :, :, left], rec_a[g].at[r], a_next)
-        start(unit, "a1-", dst.at[r, a2, :, :, right], rec_b[g].at[r], a_prev)
-        start(unit, "a2+R", dst.at[r, a1, :, :, right], rec_l[g].at[r, :, :, right], a_next)
-        start(unit, "a2-L", dst.at[r, a3, :, :, left], rec_r[g].at[r, :, :, left], a_prev)
+        start(unit, "a1", dst.at[r, a2, :, :, left], rec_in[g].at[r, :, :, left], a_next)
+        start(unit, "a1", dst.at[r, a2, :, :, right], rec_in[g].at[r, :, :, right], a_prev)
+        start(unit, "a2", dst.at[r, a1, :, :, right], rec_out[g].at[r, 0, :, :, right], a_next)
+        start(unit, "a2", dst.at[r, a3, :, :, left], rec_out[g].at[r, 1, :, :, left], a_prev)
 
     def stage1(unit):
         r, g = unit
         left, right = RS_LEFT[g], RS_RIGHT[g]
-        ref, from_a, from_b = part[g], rec_a[g], rec_b[g]
-        arrived(unit, "a1+", "a1-")
+        ref, held = part[g], rec_in[g]
+        arrived(unit, "a1", held.at[r])
 
         def put_left(i, n, width, value):
             ref[r, a1, i, :, pl.ds(n, width)] = value
@@ -234,9 +231,9 @@
         add(
             4, 0, left.size, put_left,
             lambda i, n, width: ref[r, a1, i, :, pl.ds(n, width)],
-            lambda i, n, width: from_a[r, i, :, pl.ds(n, width)],
+            lambda i, n, width: held[r, i, :, pl.ds(n, width)],
         )
-        start(unit, "a2+L", ref.at[r, a1, :, :, left], rec_l[g].at[r, :, :, left], a_next)
+        start(unit, "a2", ref.at[r, a1, :, :, left], rec_out[g].at[r, 0, :, :, left], a_next)
 
         def put_right(i, n, width, value):
             ref[r, a3, i, :, pl.ds(n, width)] = value
@@ -244,15 +241,15 @@
         add(
             4, right.start, right.size, put_right,
             lambda i, n, width: ref[r, a3, i, :, pl.ds(n, width)],
-            lambda i, n, width: from_b[r, i, :, pl.ds(n - right.start, width)],
+            lambda i, n, width: held[r, i, :, pl.ds(n, width)],
         )
-        start(unit, "a2-R", ref.at[r, a3, :, :, right], rec_r[g].at[r, :, :, right], a_prev)
+        start(unit, "a2", ref.at[r, a3, :, :, right], rec_out[g].at[r, 1, :, :, right], a_prev)
 
     def stage2(unit):
         r, g = unit
         left, right = RS_LEFT[g], RS_RIGHT[g]
-        ref, from_l, from_r, to = part[g], rec_l[g], rec_r[g], summed[g]
-        arrived(unit, "a2+R", "a2-L", "a2+L", "a2-R")
+        ref, held, to = part[g], rec_out[g], summed[g]
+        arrived(unit, "a2", held.at[r])
 
         def put(i, n, width, value):
             to[r, i, :, pl.ds(n, width)] = value
@@ -260,34 +257,34 @@
         add(
             4, 0, left.size + right.size, put,
             lambda i, n, width: ref[r, a, i, :, pl.ds(n, width)],
-            lambda i, n, width: from_l[r, i, :, pl.ds(n, width)],
-            lambda i, n, width: from_r[r, i, :, pl.ds(n, width)],
+            lambda i, n, width: held[r, 0, i, :, pl.ds(n, width)],
+            lambda i, n, width: held[r, 1, i, :, pl.ds(n, width)],
         )
-        start(unit, "b1+", to.at[r, b2, :, left], sec_a[g].at[r], b_next)
-        start(unit, "b1-", to.at[r, b2, :, right], sec_b[g].at[r], b_prev)
-        start(unit, "b2+R", to.at[r, b1, :, right], sec_l[g].at[r, :, right], b_next)
-        start(unit, "b2-L", to.at[r, b3, :, left], sec_r[g].at[r, :, left], b_prev)
+        start(unit, "b1", to.at[r, b2, :, left], sec_in[g].at[r, :, left], b_next)
+        start(unit, "b1", to.at[r, b2, :, right], sec_in[g].at[r, :, right], b_prev)
+        start(unit, "b2", to.at[r, b1, :, right], sec_out[g].at[r, 0, :, right], b_next)
+        start(unit, "b2", to.at[r, b3, :, left], sec_out[g].at[r, 1, :, left], b_prev)
 
     def stage3(unit):
         r, g = unit
         left, right = RS_LEFT[g], RS_RIGHT[g]
         ref = summed[g]
-        arrived(unit, "b1+", "b1-")
-        value = ref[r, b1, :, left].astype(F32) + sec_a[g][r].astype(F32)
+        arrived(unit, "b1", sec_in[g].at[r])
+        value = ref[r, b1, :, left].astype(F32) + sec_in[g][r, :, left].astype(F32)
         ref[r, b1, :, left] = value.astype(BF)
-        start(unit, "b2+L", ref.at[r, b1, :, left], sec_l[g].at[r, :, left], b_next)
-        value = ref[r, b3, :, right].astype(F32) + sec_b[g][r].astype(F32)
+        start(unit, "b2", ref.at[r, b1, :, left], sec_out[g].at[r, 0, :, left], b_next)
+        value = ref[r, b3, :, right].astype(F32) + sec_in[g][r, :, right].astype(F32)
         ref[r, b3, :, right] = value.astype(BF)
-        start(unit, "b2-R", ref.at[r, b3, :, right], sec_r[g].at[r, :, right], b_prev)
+        start(unit, "b2", ref.at[r, b3, :, right], sec_out[g].at[r, 1, :, right], b_prev)
 
     def stage4(unit):
         r, g = unit
-        arrived(unit, "b2+R", "b2-L", "b2+L", "b2-R")
+        arrived(unit, "b2", sec_out[g].at[r])
 
         def total(k):
             cols = pl.ds(k * HALF, HALF)
-            value = summed[g][r, b, :, cols].astype(F32) + sec_l[g][r, :, cols].astype(F32)
-            return (value + sec_r[g][r, :, cols].astype(F32)).astype(BF)
+            value = summed[g][r, b, :, cols].astype(F32) + sec_out[g][r, 0, :, cols].astype(F32)
+            return (value + sec_out[g][r, 1, :, cols].astype(F32)).astype(BF)
 
         low, high = pl.ds(0, HALF), pl.ds(HALF, HALF)
         if g == 0:
@@ -301,43 +298,44 @@
             sig = jax.nn.sigmoid(gate)
             own[1][r, a, b, :, low] = (grad * up * sig * (1.0 + gate * (1.0 - sig))).astype(BF)
             own[1][r, a, b, :, high] = (grad * gate * sig).astype(BF)
-        start(unit, "c1+", own[g].at[r, a, b], own[g].at[r, a, b], b_next)
-        start(unit, "c1-", own[g].at[r, a, b], own[g].at[r, a, b], b_prev)
+        start(unit, "c1", own[g].at[r, a, b], own[g].at[r, a, b], b_next)
+        start(unit, "c1", own[g].at[r, a, b], own[g].at[r, a, b], b_prev)
 
     def stage5(unit):
         r, g = unit
         left, right = AG_LEFT[g], AG_RIGHT[g]
-        arrived(unit, "c1+", "c1-")
-        start(unit, "c2+", own[g].at[r, a, b3, :, left], own[g].at[r, a, b3, :, left], b_next)
-        start(unit, "c2-", own[g].at[r, a, b1, :, right], own[g].at[r, a, b1, :, right], b_prev)
-
-    def share(unit, name, k):
-        r, g = unit
-        start(unit, name, own[g].at[r, k], other[g].at[r, :, k], partner)
+        arrived(unit, "c1", own[g].at[r, a, pl.ds(0, 2)])
+        start(unit, "c2", own[g].at[r, a, b3, :, left], own[g].at[r, a, b3, :, left], b_next)
+        start(unit, "c2", own[g].at[r, a, b1, :, right], own[g].at[r, a, b1, :, right], b_prev)
+
+    def share(unit, k):
+        r, g = unit
+        start(unit, "s", own[g].at[r, k], other[g].at[r, :, k], partner)
 
     def stage6(unit):
         r, g = unit
-        arrived(unit, "c2+", "c2-")
-        start(unit, "d1+", own[g].at[r, a], own[g].at[r, a], a_next)
-        start(unit, "d1-", own[g].at[r, a], own[g].at[r, a], a_prev)
-        share(unit, "s0", a)
+        arrived(unit, "c2", own[g].at[r, a, b2])
+        start(unit, "d1", own[g].at[r, a], own[g].at[r, a], a_next)
+        start(unit, "d1", own[g].at[r, a], own[g].at[r, a], a_prev)
+        share(unit, a)
 
     def stage7(unit):
         r, g = unit
         left, right = AG_LEFT[g], AG_RIGHT[g]
-        arrived(unit, "d1+", "d1-")
-        start(unit, "d2+", own[g].at[r, a3, :, :, left], own[g].at[r, a3, :, :, left], a_next)
-        start(unit, "d2-", own[g].at[r, a1, :, :, right], own[g].at[r, a1, :, :, right], a_prev)
-        share(unit, "s1", a1)
-        share(unit, "s3", a3)
+        arrived(unit, "d1", own[g].at[r, pl.ds(0, 2)])
+        start(unit, "d2", own[g].at[r, a3, :, :, left], own[g].at[r, a3, :, :, left], a_next)
+        start(unit, "d2", own[g].at[r, a1, :, :, right], own[g].at[r, a1, :, :, right], a_prev)
+        share(unit, a1)
+        share(unit, a3)
 
     def stage8(unit):
-        arrived(unit, "d2+", "d2-")
-        share(unit, "s2", a2)
+        r, g = unit
+        arrived(unit, "d2", own[g].at[r, a2])
+        share(unit, a2)
 
     def stage9(unit):
         r, g = unit
-        arrived(unit, "s0", "s1", "s3", "s2")
+        arrived(unit, "s", other[g].at[r])
         ours, rest = flat(own[g][r]), flat(other[g][r])
         if g == 0:
             use("theirs_down")
@@ -348,14 +346,14 @@
         z_part[g, r] = total.astype(BF).reshape((RING, RING, ROWS, WIDTH))
         if unit not in TREE:
             for j in (4, 3, 5, 2, 6, 1, 7):
-                start(unit, f"e{j}", piece(z_part, unit, j), z_rec.at[g, r, j - 1], others[j - 1])
+                start(unit, "e1", piece(z_part, unit, j), z_rec.at[g, r, j - 1], others[j - 1])
             return
-        start(unit, "e3", piece(z_part, unit, 5), z_rec.at[g, r, 2], others[6])
-        start(unit, "e5", piece(z_part, unit, 3), z_rec.at[g, r, 3], others[0])
-        start(unit, "e4a", piece(z_part, unit, 4).at[0], z_rec.at[g, r, 4, 0], others[5])
-        start(unit, "e4b", piece(z_part, unit, 4).at[1], z_rec.at[g, r, 4, 1], others[1])
-        start(unit, "e1", piece(z_part, unit, 1), z_rec.at[g, r, 0], others[0])
-        start(unit, "e7", piece(z_part, unit, 7), z_rec.at[g, r, 1], others[6])
+        start(unit, "e1", piece(z_part, unit, 5), z_rec.at[g, r, 0], others[6])
+        start(unit, "e1", piece(z_part, unit, 3), z_rec.at[g, r, 1], others[0])
+        start(unit, "e1", piece(z_part, unit, 4).at[0], z_rec.at[g, r, 2, 0], others[5])
+        start(unit, "e1", piece(z_part, unit, 4).at[1], z_rec.at[g, r, 2, 1], others[1])
+        start(unit, "e2", piece(z_part, unit, 1), z_rec.at[g, r, 3], others[0])
+        start(unit, "e2", piece(z_part, unit, 7), z_rec.at[g, r, 4], others[6])
 
     def piece(ref, unit, by):
         r, g = unit
@@ -364,15 +362,15 @@
 
     def stage15(unit):
         r, g = unit
-        arrived(unit, "e3", "e5", "e4a", "e4b")
-        for by, slot, half in ((6, 2, 0), (2, 3, 1)):
+        arrived(unit, "e1", z_rec.at[g, r, pl.ds(0, 3)])
+        for by, slot, half in ((6, 0, 0), (2, 1, 1)):
             here = piece(z_part, unit, by)
             total = here[...].astype(F32) + z_rec[g, r, slot].astype(F32)
             both = [total[0], total[1]]
-            both[half] = both[half] + z_rec[g, r, 4, half].astype(F32)
+            both[half] = both[half] + z_rec[g, r, 2, half].astype(F32)
             here[0] = both[0].astype(BF)
             here[1] = both[1].astype(BF)
-        start(unit, "e6", piece(z_part, unit, 6), z_rec.at[g, r, 5], others[5])
+        start(unit, "e2", piece(z_part, unit, 6), z_rec.at[g, r, 5], others[5])
         start(unit, "e2", piece(z_part, unit, 2), z_rec.at[g, r, 6], others[1])
 
     def stage10(unit):
@@ -380,30 +378,32 @@
         tree = unit in TREE
         total = piece(z_part, unit, 0)[...].astype(F32)
         if tree:
-            arrived(unit, "e1", "e7", "e2", "e6")
+            arrived(unit, "e2", z_rec.at[g, r, pl.ds(3, 4)])
         else:
-            arrived(unit, *[f"e{j}" for j in range(1, N_Z)])
-        for j in (0, 1, 5, 6) if tree else range(N_Z - 1):
+            arrived(unit, "e1", z_rec.at[g, r])
+        for j in (3, 4, 5, 6) if tree else range(N_Z - 1):
             total = total + z_rec[g, r, j].astype(F32)
         here = piece(z_sum, unit, 0)
         here[...] = total.astype(BF)
         for j in (2, 6, 1, 7) if tree else (4, 3, 5, 2, 6, 1, 7):
-            start(unit, f"f{j}", here, here, others[j - 1])
+            start(unit, "f1" if j in (2, 6) or not tree else "f2", here, here, others[j - 1])
 
     def stage16(unit):
-        arrived(unit, "f2", "f6")
+        r, g = unit
+        arrived(unit, "f1", z_rec.at[g, r, pl.ds(0, 2)])
         far = piece(z_sum, unit, 6)
-        start(unit, "f3", far, far, others[0])
-        start(unit, "f4a", far.at[0], far.at[0], others[1])
+        start(unit, "f2", far, far, others[0])
+        start(unit, "f2", far.at[0], far.at[0], others[1])
         far = piece(z_sum, unit, 2)
-        start(unit, "f5", far, far, others[6])
-        start(unit, "f4b", far.at[1], far.at[1], others[5])
+        start(unit, "f2", far, far, others[6])
+        start(unit, "f2", far.at[1], far.at[1], others[5])
 
     def stage11(unit):
+        r, g = unit
         if unit in TREE:
-            arrived(unit, "f1", "f7", "f3", "f5", "f4a", "f4b")
+            arrived(unit, "f2", z_rec.at[g, r, pl.ds(0, 5)])
         else:
-            arrived(unit, *[f"f{j}" for j in range(1, N_Z)])
+            arrived(unit, "f1", z_rec.at[g, r])
 
     def tall(held, cols):
         return held[:, :, :, :, cols].reshape((CHUNKS * BLOCK, cols.size))
@@ -437,8 +437,17 @@
         stages[i]((r, g))
     for copy in swaps:
         copy.wait_send()
-    for copy in flows.values():
-        copy.wait_send()
+
+    def all_sent(i, ref):
+        remote(ref, ref, send.at[i], recv.at[0, 0], partner).wait_send()
+
+    for g in range(2):
+        all_sent(g, z_rec)
+        all_sent(2 + g, part[g].at[:, pl.ds(0, 3)])
+        all_sent(4 + g, part[g].at[:, 0, pl.ds(0, 3)])
+        all_sent(6 + g, own[g].at[:, 0, pl.ds(0, 3)])
+        all_sent(8 + g, own[g].at[:, pl.ds(0, 3)])
+        all_sent(10 + g, own[g])
     use(*list(waits))
 
 
@@ -493,19 +502,17 @@
             V((2, HALF, WIDTH), BF), V((HALF, WIDTH), BF),
             V((WIDTH, CHUNKS * BLOCK), BF), V((WIDTH, CHUNKS * BLOCK), BF),
             pair(grad, (2 * HALF, HALF)),
-            pair((CHUNKS, RING, ROWS), (896, 512)),
-            pair((CHUNKS, RING, ROWS), (896, 384)),
-            pair((CHUNKS, RING, ROWS), (2 * HALF, HALF)), pair((CHUNKS, RING, ROWS), (2 * HALF, HALF)),
             pair((CHUNKS, RING, ROWS), (2 * HALF, HALF)),
-            pair((CHUNKS, ROWS), (896, 512)), pair((CHUNKS, ROWS), (896, 384)),
-            pair((CHUNKS, ROWS), (2 * HALF, HALF)), pair((CHUNKS, ROWS), (2 * HALF, HALF)),
+            pair((CHUNKS, 2, RING, ROWS), (2 * HALF, HALF)),
+            pair((CHUNKS, RING, ROWS), (2 * HALF, HALF)),
+            pair((CHUNKS, ROWS), (2 * HALF, HALF)),
+            pair((CHUNKS, 2, ROWS), (2 * HALF, HALF)),
             V((CHUNKS, ROWS, 2 * HALF), BF),
             pair(grad, (HALF, 2 * HALF)), pair(grad, (HALF, 2 * HALF)),
             V((2,) + rows, BF),
             V((2, CHUNKS, N_Z - 1, 2, ROWS, WIDTH), BF),
-            pltpu.SemaphoreType.DMA((2 * CHUNKS, N_SEMS)), pltpu.SemaphoreType.DMA((2 * CHUNKS, N_SEMS)),
-            pltpu.SemaphoreType.DMA((8,)), pltpu.SemaphoreType.DMA((8,)),
-            pltpu.SemaphoreType.DMA((24,)),
+            pltpu.SemaphoreType.DMA((12,)), pltpu.SemaphoreType.DMA((len(KINDS), 2 * CHUNKS)),
+            pltpu.SemaphoreType.DMA((7,)), pltpu.SemaphoreType.DMA((7,)), pltpu.SemaphoreType.DMA((10,)),
         ],
         compiler_params=pltpu.CompilerParams(
             collective_id=0, has_side_effects=True, vmem_limit_bytes=60 << 20

time: 110 us -> 105 us (0.955)
  Pallas kernels: 106 us -> 100 us
    pallas_call x1, Pallas kernels: 102 us -> 96.5 us  [per_device(): pl.pallas_call(kernel, out_shape=(V((2,) + rows, BF), V((2, WIDTH, 2 * HA...]
where the time goes in v3:
time: 105 us; the launch traced here: 104 us
  Pallas kernels  100 us (95%)
  local copies, waits for them, and re-layouts  3.17 us (3%)
    pallas_call x1, Pallas kernels, per_device(): pl.pallas_call(kernel, out_shape=(V((2,) + rows, BF), V((2, WIDTH, 2 * HA...  96.5 us
    pallas_call x1, Pallas kernels, per_device(): pl.pallas_call(write_out, out_shape=(S(rows, BF), S(rows, BF), S((WIDTH,...  3.97 us
    unnamed x6, local copies, waits for them, and re-layouts  3.17 us

profile of v3, /device:TPU:1, one launch (start us, length us, event | category | flops | bytes accessed | tf_op | source)
XLA Modules:
  0.0 104.4 jit_solution(6183534923087798713)
XLA Ops:
  0.6 96.5 %shard_map.92 = (bf16[2,4,4,4,16,256]{5,4,3,2,1,0:T(8,128)(2,1)S(1)}, bf16[2,256,1792]{2,1,0:T(8,128)(2,1)S(1)}, bf16[2,896,256]{2,1,0:T(8,128)(2,1)S(1)}) custom-call(bf16[4,4,4,16,256]{4,3,2,1,0:T(8,128)(2,1)} %bitcast.7, bf16[256,1792]{1,0:T(8,128)(2,1)} %gw_in.1, bf16[256,1792]{1,0:T(8,128)(2,1)} %uw_in.1, bf16[2,896,256]{2,1,0:T(8,128)(2,1)} %bitcast.6, ...), custom_call_target="tpu_custom_call" | custom-call | tf_op jit(solution)/shard_map/pallas_call | solution.py:494
  97.1 0.0 copy-start
  97.1 1.2 %copy-done = bf16[2,256,1792]{2,1,0:T(8,128)(2,1)} copy-done((bf16[2,256,1792]{2,1,0:T(8,128)(2,1)}, bf16[2,256,1792]{2,1,0:T(8,128)(2,1)S(1)}, u32[]{:S(2)}) %copy-start) | copy-done | bytes 1835032
  98.4 0.0 copy-start.1
  98.4 1.0 copy-done.1
  99.3 0.0 copy-start.2
  99.3 0.9 copy-done.2
  100.3 4.0 %shard_map.93 = (bf16[4,4,4,16,256]{4,3,2,1,0:T(8,128)(2,1)}, bf16[4,4,4,16,256]{4,3,2,1,0:T(8,128)(2,1)}, bf16[256,1792]{1,0:T(8,128)(2,1)}, bf16[256,1792]{1,0:T(8,128)(2,1)}, bf16[2,896,256]{2,1,0:T(8,128)(2,1)}) custom-call(bf16[2,4,4,4,16,256]{5,4,3,2,1,0:T(8,128)(2,1)} %copy-done.1, bf16[2,256,1792]{2,1,0:T(8,128)(2,1)} %copy-done, ...), custom_call_target="tpu_custom_call" | custom-call | tf_op jit(solution)/shard_map/pallas_call | solution.py:523
Async XLA Ops:
  97.1 1.3 %copy-start = (bf16[2,256,1792]{2,1,0:T(8,128)(2,1)}, bf16[2,256,1792]{2,1,0:T(8,128)(2,1)S(1)}, u32[]{:S(2)}) copy-start(bf16[2,256,1792]{2,1,0:T(8,128)(2,1)S(1)} %get-tuple-element.14.grads) | copy-start | bytes 5505028
  98.4 1.0 copy-start.1
  99.3 0.9 copy-start.2

commit v4 on v3

--- a/solution.py
+++ b/solution.py
@@ -12,9 +12,10 @@
 CHUNKS, RING, ROWS, N_Z = 4, 4, 16, 8
 BLOCK = RING * RING * ROWS
 WIDTH, HALF = 256, 896
+FAR_B, FAR_C, FAR_A = (), (), ()
 KINDS = ("a1", "a2", "b1", "b2", "c1", "c2", "d1", "d2", "s", "e1", "e2", "f1", "f2")
 SENDS = "efabcds"
-TREE = {(0, 1), (2, 1), (0, 0), (1, 1), (2, 0), (3, 0), (1, 0)}
+TREE = ((0, 0), (0, 1), (1, 0), (1, 1), (2, 0), (2, 1), (3, 0))
 Z_PEERS = (1, 2, 3, 4, 5, 6, 7)
 RS_LEFT, RS_RIGHT = (pl.ds(0, 896), pl.ds(0, 512)), (pl.ds(896, 896), pl.ds(512, 384))
 AG_LEFT, AG_RIGHT = (pl.ds(0, 512), pl.ds(0, 896)), (pl.ds(512, 384), pl.ds(896, 896))
@@ -71,6 +72,7 @@
         )
 
     a_next, a_prev, b_next, b_prev = step_a(1), step_a(-1), step_b(1), step_b(-1)
+    a_far, b_far = step_a(2), step_b(2)
     partner = (y * 8 + x * 2 + 1 - core, z)
     others = [(row, (z + j) % N_Z) for j in range(1, N_Z)]
     a1, a2, a3 = (a + 1) % 4, (a + 2) % 4, (a + 3) % 4
@@ -118,7 +120,8 @@
     load_rows("cot0", cot_in, cot, 0, 1)
 
     barrier = pltpu.get_barrier_semaphore()
-    peers = [partner, a_next, a_prev, b_next, b_prev] + [others[j - 1] for j in Z_PEERS]
+    peers = [partner, a_next, a_prev, b_next, b_prev] + [a_far] * bool(FAR_A) + [b_far] * bool(FAR_B + FAR_C)
+    peers += [others[j - 1] for j in Z_PEERS]
     for peer in peers:
         pl.semaphore_signal(barrier, inc=1, device_id=peer, device_id_type=MESH)
     pl.semaphore_wait(barrier, len(peers))
@@ -260,6 +263,11 @@
             lambda i, n, width: held[r, 0, i, :, pl.ds(n, width)],
             lambda i, n, width: held[r, 1, i, :, pl.ds(n, width)],
         )
+        if unit in FAR_B:
+            start(unit, "b1", to.at[r, b2], sec_in[g].at[r], b_far)
+            start(unit, "b2", to.at[r, b1], sec_out[g].at[r, 0], b_next)
+            start(unit, "b2", to.at[r, b3], sec_out[g].at[r, 1], b_prev)
+            return
         start(unit, "b1", to.at[r, b2, :, left], sec_in[g].at[r, :, left], b_next)
         start(unit, "b1", to.at[r, b2, :, right], sec_in[g].at[r, :, right], b_prev)
         start(unit, "b2", to.at[r, b1, :, right], sec_out[g].at[r, 0, :, right], b_next)
@@ -279,12 +287,17 @@
 
     def stage4(unit):
         r, g = unit
+        if unit in FAR_B:
+            arrived(unit, "b1", sec_in[g].at[r])
         arrived(unit, "b2", sec_out[g].at[r])
 
         def total(k):
             cols = pl.ds(k * HALF, HALF)
             value = summed[g][r, b, :, cols].astype(F32) + sec_out[g][r, 0, :, cols].astype(F32)
-            return (value + sec_out[g][r, 1, :, cols].astype(F32)).astype(BF)
+            value = value + sec_out[g][r, 1, :, cols].astype(F32)
+            if unit in FAR_B:
+                value = value + sec_in[g][r, :, cols].astype(F32)
+            return value.astype(BF)
 
         low, high = pl.ds(0, HALF), pl.ds(HALF, HALF)
         if g == 0:
@@ -300,6 +313,8 @@
             own[1][r, a, b, :, high] = (grad * gate * sig).astype(BF)
         start(unit, "c1", own[g].at[r, a, b], own[g].at[r, a, b], b_next)
         start(unit, "c1", own[g].at[r, a, b], own[g].at[r, a, b], b_prev)
+        if unit in FAR_C:
+            start(unit, "c2", own[g].at[r, a, b], own[g].at[r, a, b], b_far)
 
     def stage5(unit):
         r, g = unit
@@ -314,17 +329,22 @@
 
     def stage6(unit):
         r, g = unit
+        if unit in FAR_C:
+            arrived(unit, "c1", own[g].at[r, a, pl.ds(0, 2)])
         arrived(unit, "c2", own[g].at[r, a, b2])
         start(unit, "d1", own[g].at[r, a], own[g].at[r, a], a_next)
         start(unit, "d1", own[g].at[r, a], own[g].at[r, a], a_prev)
+        if unit in FAR_A:
+            start(unit, "d2", own[g].at[r, a], own[g].at[r, a], a_far)
         share(unit, a)
 
     def stage7(unit):
         r, g = unit
         left, right = AG_LEFT[g], AG_RIGHT[g]
         arrived(unit, "d1", own[g].at[r, pl.ds(0, 2)])
-        start(unit, "d2", own[g].at[r, a3, :, :, left], own[g].at[r, a3, :, :, left], a_next)
-        start(unit, "d2", own[g].at[r, a1, :, :, right], own[g].at[r, a1, :, :, right], a_prev)
+        if unit not in FAR_A:
+            start(unit, "d2", own[g].at[r, a3, :, :, left], own[g].at[r, a3, :, :, left], a_next)
+            start(unit, "d2", own[g].at[r, a1, :, :, right], own[g].at[r, a1, :, :, right], a_prev)
         share(unit, a1)
         share(unit, a3)
 
@@ -528,6 +548,7 @@
         in_specs=[vmem] * 3,
         out_specs=[hbm] * 5,
         scratch_shapes=[pltpu.SemaphoreType.DMA((8,))],
+        compiler_params=pltpu.CompilerParams(vmem_limit_bytes=1 << 20),
     )(*results)
     return (
         output.reshape(tokens.shape), tokens_grad.reshape(tokens.shape), gate_grad, up_grad,

time: 105 us -> 99.3 us (0.946)
  local copies, waits for them, and re-layouts: 3.17 us -> 0 us
  Pallas kernels: 100 us -> 98.4 us
    unnamed x6 -> x0, local copies, waits for them, and re-layouts: 3.17 us -> none
    pallas_call x1, Pallas kernels: 3.97 us -> 1.95 us  [per_device(): pl.pallas_call(write_out, out_shape=(S(rows, BF), S(rows, BF), S((WIDTH,...]
where the time goes in v4:
time: 99.3 us; the launch traced here: 99.2 us
  Pallas kernels  98.4 us (99%)
    pallas_call x1, Pallas kernels, per_device(): pl.pallas_call(kernel, out_shape=(V((2,) + rows, BF), V((2, WIDTH, 2 * HA...  96.5 us

profile of v4, /device:TPU:1, one launch (start us, length us, event | category | flops | bytes accessed | tf_op | source)
XLA Modules:
  0.0 99.2 jit_solution(6028328396401195704)
XLA Ops:
  0.6 96.5 %shard_map.92 = (bf16[2,4,4,4,16,256]{5,4,3,2,1,0:T(8,128)(2,1)S(1)}, bf16[2,256,1792]{2,1,0:T(8,128)(2,1)S(1)}, bf16[2,896,256]{2,1,0:T(8,128)(2,1)S(1)}) custom-call(bf16[4,4,4,16,256]{4,3,2,1,0:T(8,128)(2,1)} %bitcast.7, bf16[256,1792]{1,0:T(8,128)(2,1)} %gw_in.1, bf16[256,1792]{1,0:T(8,128)(2,1)} %uw_in.1, bf16[2,896,256]{2,1,0:T(8,128)(2,1)} %bitcast.6, ...), custom_call_target="tpu_custom_call" | custom-call | tf_op jit(solution)/shard_map/pallas_call | solution.py:514
  97.1 1.9 %shard_map.93 = (bf16[4,4,4,16,256]{4,3,2,1,0:T(8,128)(2,1)}, bf16[4,4,4,16,256]{4,3,2,1,0:T(8,128)(2,1)}, bf16[256,1792]{1,0:T(8,128)(2,1)}, bf16[256,1792]{1,0:T(8,128)(2,1)}, bf16[2,896,256]{2,1,0:T(8,128)(2,1)}) custom-call(bf16[2,4,4,4,16,256]{5,4,3,2,1,0:T(8,128)(2,1)S(1)} %get-tuple-element.13.z_sum, ...), custom_call_target="tpu_custom_call" | custom-call | tf_op jit(solution)/shard_map/pallas_call | solution.py:543

commit v5 on v4

--- a/solution.py
+++ b/solution.py
@@ -33,9 +33,10 @@
     (9, 1, 1), (10, 0, 1), (10, 1, 0), (7, 2, 1), (8, 2, 0), (16, 0, 0), (7, 3, 0), (9, 2, 0),
     (6, 3, 1), (15, 1, 1), (16, 0, 1), (8, 2, 1), (16, 1, 0), (8, 3, 0), (9, 2, 1), (11, 0, 0),
     (9, 3, 0), (15, 2, 0), (12, 0, 0), (7, 3, 1), (10, 1, 1), (11, 0, 1), (11, 1, 0), (12, 1, 0),
-    (15, 2, 1), (15, 3, 0), (8, 3, 1), (10, 2, 0), (16, 1, 1), (9, 3, 1), (10, 2, 1), (13, 0, 1),
-    (10, 3, 0), (16, 2, 0), (11, 1, 1), (13, 1, 1), (10, 3, 1), (16, 2, 1), (16, 3, 0), (11, 2, 0),
-    (11, 3, 1), (11, 2, 1), (11, 3, 0),]
+    (15, 2, 1), (15, 3, 0), (8, 3, 1), (10, 2, 0), (16, 1, 1), (9, 3, 1), (10, 2, 1), (10, 3, 0),
+    (16, 2, 0), (11, 1, 1), (10, 3, 1), (16, 2, 1), (16, 3, 0), (13, 1, 1), (13, 0, 1), (11, 2, 0),
+    (11, 3, 1), (11, 2, 1), (11, 3, 0),
+]
 
 
 def dot(left, right):
@@ -198,26 +199,32 @@
     def stage0(unit):
         r, g = unit
         late = "" if r == 0 else "1"
+        dst = part[g]
         if g == 0:
-            use("tok0", "mine_gate", "mine_up", "tok_p0", "gate_p", "up_p", "tok" + late, "tok_p" + late)
+            use("tok0", "tok_p0", "tok" + late, "tok_p" + late)
+            mine, theirs = flat(tok[r]), flat(tok_p[r])
         else:
             use("cot0", "mine_down", "cot_p0", "down_p", "cot" + late, "cot_p" + late)
-        dst = part[g]
+            mine, theirs = flat(cot[r]), flat(cot_p[r])
+
+        def project(side):
+            for n in range(side.start, side.start + side.size, 256):
+                size = min(256, side.start + side.size - n)
+                cols = pl.ds(n, size)
+                if g == 0:
+                    total = dot(mine, gu[core, :, cols]) + dot(theirs, gu_p[:, cols])
+                else:
+                    total = dot_t(mine, dw[core, cols, :]) + dot_t(theirs, dw_p[cols, :])
+                dst[r, :, :, :, cols] = total.astype(BF).reshape((RING, RING, ROWS, size))
+
+        left, right = RS_LEFT[g], RS_RIGHT[g]
         if g == 0:
-            t, tp = flat(tok[r]), flat(tok_p[r])
-            for n in range(0, 2 * HALF, 256):
-                cols = pl.ds(n, 256)
-                total = dot(t, gu[core, :, cols]) + dot(tp, gu_p[:, cols])
-                dst[r, :, :, :, cols] = total.astype(BF).reshape((RING, RING, ROWS, 256))
-        else:
-            c, cp = flat(cot[r]), flat(cot_p[r])
-            for n in range(0, HALF, 256):
-                size = min(256, HALF - n)
-                units = pl.ds(n, size)
-                total = dot_t(c, dw[core, units, :]) + dot_t(cp, dw_p[units, :])
-                dst[r, :, :, :, units] = total.astype(BF).reshape((RING, RING, ROWS, size))
-        left, right = RS_LEFT[g], RS_RIGHT[g]
+            use("mine_gate", "gate_p")
+        project(left)
         start(unit, "a1", dst.at[r, a2, :, :, left], rec_in[g].at[r, :, :, left], a_next)
+        if g == 0:
+            use("mine_up", "up_p")
+        project(right)
         start(unit, "a1", dst.at[r, a2, :, :, right], rec_in[g].at[r, :, :, right], a_prev)
         start(unit, "a2", dst.at[r, a1, :, :, right], rec_out[g].at[r, 0, :, :, right], a_next)
         start(unit, "a2", dst.at[r, a3, :, :, left], rec_out[g].at[r, 1, :, :, left], a_prev)

time: 99.3 us -> 98.6 us (level)
  no operation moved by 1% of the time
where the time goes in v5:
time: 98.6 us
  Pallas kernels  97.8 us (99%)
    pallas_call x1, Pallas kernels, per_device(): pl.pallas_call(kernel, out_shape=(V((2,) + rows, BF), V((2, WIDTH, 2 * HA...  95.8 us

profile of v5, /device:TPU:1, one launch (start us, length us, event | category | flops | bytes accessed | tf_op | source)
XLA Modules:
  0.0 98.6 jit_solution(16083768453677389261)
XLA Ops:
  0.6 95.8 %shard_map.92 = (bf16[2,4,4,4,16,256]{5,4,3,2,1,0:T(8,128)(2,1)S(1)}, bf16[2,256,1792]{2,1,0:T(8,128)(2,1)S(1)}, bf16[2,896,256]{2,1,0:T(8,128)(2,1)S(1)}) custom-call(bf16[4,4,4,16,256]{4,3,2,1,0:T(8,128)(2,1)} %bitcast.7, bf16[256,1792]{1,0:T(8,128)(2,1)} %gw_in.1, bf16[256,1792]{1,0:T(8,128)(2,1)} %uw_in.1, bf16[2,896,256]{2,1,0:T(8,128)(2,1)} %bitcast.6, ...), custom_call_target="tpu_custom_call" | custom-call | tf_op jit(solution)/shard_map/pallas_call | solution.py:521
  96.5 1.9 %shard_map.93 = (bf16[4,4,4,16,256]{4,3,2,1,0:T(8,128)(2,1)}, bf16[4,4,4,16,256]{4,3,2,1,0:T(8,128)(2,1)}, bf16[256,1792]{1,0:T(8,128)(2,1)}, bf16[256,1792]{1,0:T(8,128)(2,1)}, bf16[2,896,256]{2,1,0:T(8,128)(2,1)}) custom-call(bf16[2,4,4,4,16,256]{5,4,3,2,1,0:T(8,128)(2,1)S(1)} %get-tuple-element.13.z_sum, ...), custom_call_target="tpu_custom_call" | custom-call | tf_op jit(solution)/shard_map/pallas_call | solution.py:550
